TPU v7x, 32 devices: a whole 2x2x4 slice. The times are simulated.
32 devices in a mesh: sector: 8 (over y, x, core), block: 4 (over z).
Axes of the slice: x: 2, y: 2, z: 4, core: 2. Of those that a mesh axis runs over, the one named last changes fastest.
Arguments:
- flow: float32 [5, 4, 64, 1024], P(None, None, 'block', 'sector'), may hold values from -1 to 5, as said below
- adjoint: float32 [5, 4, 64, 1024], P(None, None, 'block', 'sector'), may hold values from -6 to 6
- adjoint_later: float32 [2, 5, 4, 64, 1024], P(None, None, None, 'block', 'sector'), may hold values from -6 to 6
- objective_grad: float32 [5, 4, 64, 1024], P(None, None, 'block', 'sector'), may hold values from -12 to 12
- volume: float32 [4, 64, 1024], P(None, 'block', 'sector'), may hold values from 0.5 to 2
- panel_maps: float32 [4, 4, 128, 128], replicated, may hold values from 0 to 1, as said below
- rotor_step: int32 [1], replicated, may hold values from 0 to 31
Outputs:
- updated_adjoint: float32 [5, 4, 64, 1024], P(None, None, 'block', 'sector')
Inputs may be any that keep to these rules, and one draw needn't show every extreme that they name: `flow`: density and pressure are positive in every cell. `panel_maps`: entries are non-negative.
All inputs are finite; a program needn't handle non-finite values.
Results may differ from a plain program's by a relative error of at most 0.000057.
Values sent between devices are 32-bit elements; how exact they have to be, the bound alone decides.
No kernel may reach another device: no remote copies, remote signals or barrier semaphores. Data moves between devices by JAX's collectives and lax.ppermute only.
A program may use at most 64 MiB of HBM per device.

v0:
```python
from functools import partial

import jax
import jax.numpy as jnp
from jax import lax
from jax.experimental import pallas as pl
from jax.experimental.pallas import tpu as pltpu
from jax.sharding import PartitionSpec as P

PHASES = 4
ITERS = 4
LANES = 128
ROWS = 16
LAYERS = 4
FIELDS = 5
SEG = LANES // LAYERS

gamma_gas = 1.4
second_coef = 0.5
fourth_coef = 1.0 / 32.0
courant = 0.6
physical_step = 2.0
sensor_floor = 0.0001
highest = lax.Precision.HIGHEST

S_EVEN, B_EVEN, INLET, OUTLET, PLANE, PHASE, STATE_MAPS, GRAD_MAPS = range(8)
U1, U2, U3, HT, BX, BT, BL, CR, CP = range(9)
CELLS = 9
A2, A4, DL, ES, N0, N1 = 0, 1, 2, 7, 12, 13
FACES = 14


def up_by(x, axis, k):
    n = x.shape[axis]
    return pltpu.roll(x, (-k) % n, axis=axis)


def iota(shape, axis):
    return lax.broadcasted_iota(jnp.int32, shape, axis)


def flagged(flags, which, shape):
    return jnp.broadcast_to(flags[which], shape) == 1


def primitives(u):
    inverse = 1.0 / u[0]
    vel = [u[1] * inverse, u[2] * inverse, u[3] * inverse]
    square = vel[0] * vel[0] + vel[1] * vel[1] + vel[2] * vel[2]
    p = (gamma_gas - 1.0) * (u[4] - 0.5 * u[0] * square)
    heat = gamma_gas * p * inverse
    slow = lax.rsqrt(heat)
    sound = heat * slow
    radius, slopes = [], []
    for q in vel:
        x = q * q + 0.01
        y = lax.rsqrt(x)
        radius.append(x * y + sound)
        slopes.append(q * y * inverse)
    half = 0.5 * inverse
    cells = vel + [(u[4] + p) * inverse] + slopes + [sound * half, gamma_gas * half * slow]
    return p, radius, sound, cells


def sensor_terms(below, here, above):
    bend = above - 2.0 * here + below
    total = above + 2.0 * here + below
    inside = bend * bend + sensor_floor
    slope = lax.rsqrt(inside)
    over = 1.0 / total
    nu = inside * slope * over
    a = bend * slope * over
    b = nu * over
    return nu, -2.0 * a - 2.0 * b, a - b


def face_terms(nu_left, nu_right, rad_left, rad_right, behind, left, right, ahead):
    e2 = (0.5 * second_coef) * (nu_left + nu_right)
    ratio = fourth_coef / (fourth_coef + e2)
    e4 = fourth_coef * ratio
    slope = ratio * ratio
    lam = 0.5 * (rad_left + rad_right)
    radial, sensed = [], []
    for b, l, r, a in zip(behind, left, right, ahead):
        first = r - l
        third = a - 3.0 * first - b
        radial.append(-0.5 * (e2 * first - e4 * third))
        sensed.append((-0.25) * lam * (first + slope * third))
    return [lam * e2, lam * e4] + radial + sensed


def rolled_faces(u, p, radius, axis):
    nu, n0, n1 = sensor_terms(up_by(p, axis, -1), p, up_by(p, axis, 1))
    right = [up_by(x, axis, 1) for x in u]
    behind = [up_by(x, axis, -1) for x in u]
    ahead = [up_by(x, axis, 2) for x in u]
    return face_terms(
        nu, up_by(nu, axis, 1), radius, up_by(radius, axis, 1), behind, u, right, ahead
    ) + [n0, n1]


def dot5(a, b):
    return (a[0] * b[0] + a[1] * b[1]) + (a[2] * b[2] + a[3] * b[3]) + a[4] * b[4]


def to_state(lin, s, rbar, nbar, cells, direction):
    q = cells[direction]
    kappa = s[1] * cells[U1] + s[2] * cells[U2] + s[3] * cells[U3] + s[4] * cells[HT]
    kappa = kappa + cells[BX + direction] * rbar
    sq = s[4] * q
    pbar = nbar + sq + s[direction + 1] + cells[CP] * rbar
    scaled = (gamma_gas - 1.0) * pbar
    g = [None] * FIELDS
    square = cells[U1] * cells[U1] + cells[U2] * cells[U2] + cells[U3] * cells[U3]
    g[0] = lin[0] - q * kappa - cells[CR] * rbar + 0.5 * square * scaled
    for k in range(3):
        g[k + 1] = lin[k + 1] + q * s[k + 1] - cells[k] * scaled
    g[direction + 1] = g[direction + 1] + (s[0] + kappa)
    g[4] = lin[4] + sq + scaled
    return g


def rolled_transpose(psi, faces, cells, direction, axis, mask=None):
    w = [x - up_by(x, axis, 1) for x in psi]
    if mask is not None:
        w = [jnp.where(mask, x, 0.0) for x in w]
    gl = dot5(w, [faces(DL + k) for k in range(FIELDS)])
    ge = dot5(w, [faces(ES + k) for k in range(FIELDS)])
    a2, a4 = faces(A2), faces(A4)
    lin, s = [], []
    for x in w:
        c = a4 * x
        v = c - up_by(c, axis, -1)
        z = a2 * x + (v - up_by(v, axis, 1))
        lin.append(z - up_by(z, axis, -1))
        s.append(0.5 * (x + up_by(x, axis, -1)))
    rbar = gl + up_by(gl, axis, -1)
    nu_bar = ge + up_by(ge, axis, -1)
    v = faces(N1) * nu_bar
    nbar = faces(N0) * nu_bar + up_by(v, axis, 1) + up_by(v, axis, -1)
    return to_state(lin, s, rbar, nbar, cells, direction)


def packed_rows(tiles):
    row = iota((8, LANES), 0)
    out = tiles[0]
    for l in range(1, LAYERS):
        out = jnp.where(row >= 2 * l, pltpu.roll(tiles[l], 2 * l, axis=0), out)
    return out


def packed_quads(tiles):
    row = iota((8, LANES), 0)
    pairs = [
        jnp.where(row < 4, tiles[l], pltpu.roll(tiles[l + 1], 4, axis=0)) for l in range(0, LAYERS, 2)
    ]
    return jnp.concatenate(pairs, axis=0)


def quad(packed, l, high):
    tile = packed[8 * (l // 2) : 8 * (l // 2) + 8]
    return pltpu.roll(tile, 4, axis=0) if (l % 2 == 1) != high else tile


def pair(packed, l, to):
    shift = (to - 2 * l) % 8
    return pltpu.roll(packed, shift, axis=0) if shift else packed


def packed_strip(layers):
    lane = iota((ROWS, LANES), 1)
    out = jnp.zeros((ROWS, LANES), jnp.float32)
    for l, x in enumerate(layers):
        base = SEG * l
        out = jnp.where((lane >= base) & (lane < base + 8), pltpu.roll(x, (base + 8) % LANES, axis=1), out)
        out = jnp.where(
            (lane >= base + 24) & (lane < base + 32), pltpu.roll(x, (base + 24) % LANES, axis=1), out
        )
    return out


def packed_edges(layers, others):
    lane = iota((ROWS, LANES), 1)
    out = packed_strip(layers)
    for l, x in enumerate(others):
        base = SEG * l + 16
        out = jnp.where((lane >= base - 8) & (lane < base + 8), pltpu.roll(x, base, axis=1), out)
    return out


def from_strip(strip, l):
    lane = iota((ROWS, LANES), 1)
    base = SEG * l
    low = pltpu.roll(strip, (-(base + 24)) % LANES, axis=1)
    high = pltpu.roll(strip, (-(base + 8)) % LANES, axis=1)
    return jnp.where(lane < 8, low, jnp.where(lane >= LANES - 8, high, 0.0))


def place_in_segment():
    return jnp.bitwise_and(iota((ROWS, LANES), 1), SEG - 1)


def each(count, looped):
    def run(body):
        if looped:
            lax.fori_loop(0, count, lambda i, c: (body(i), c)[1], 0)
        else:
            for i in range(count):
                body(i)

    return run


def half_rows(half):
    return slice(8 * half, 8 * half + 8) if isinstance(half, int) else pl.ds(pl.multiple_of(8 * half, 8), 8)


def clamp(j):
    return min(max(j, 0), LAYERS - 1)


def pack_kernel(flags, flow, psi, to_t, to_a, to_b):
    even = flagged(flags, B_EVEN, (8, LANES))
    even2 = flagged(flags, B_EVEN, (16, LANES))
    for k in range(FIELDS):
        to_t[k, 0:16] = packed_edges([flow[k, l] for l in range(LAYERS)], [psi[k, l] for l in range(LAYERS)])
        low = packed_rows([flow[k, l, 0:8] for l in range(LAYERS)])
        high = packed_rows([pltpu.roll(flow[k, l, 8:16], 2, axis=0) for l in range(LAYERS)])
        to_t[k, 16:24] = jnp.where(even, low, high)
        low = packed_quads([flow[k, l, 0:8] for l in range(LAYERS)])
        high = packed_quads([pltpu.roll(flow[k, l, 8:16], 4, axis=0) for l in range(LAYERS)])
        to_a[k, 0:16] = jnp.where(even2, high, low)
        to_b[k, 0:16] = jnp.where(even2, low, high)
        low = packed_rows([psi[k, l, 0:8] for l in range(LAYERS)])
        high = packed_rows([pltpu.roll(psi[k, l, 8:16], 2, axis=0) for l in range(LAYERS)])
        to_a[k, 16:24] = jnp.where(even, high, low)
        to_b[k, 16:24] = jnp.where(even, low, high)


def mapped(near, far, maps):
    shape = near.shape
    dims = (((1,), (1,)), ((), ()))
    near = near.reshape(shape[0] * shape[1], LANES)
    far = far.reshape(shape[0] * shape[1], LANES)
    out = lax.dot_general(near, maps[0], dims, precision=highest, preferred_element_type=jnp.float32)
    out = out + lax.dot_general(far, maps[1], dims, precision=highest, preferred_element_type=jnp.float32)
    return out.reshape(shape)


def mapped_back(near, far, maps):
    shape = near.shape
    both = jnp.concatenate([near, far], axis=2).reshape(shape[0] * shape[1], 2 * LANES)
    table = maps[...].reshape(2 * LANES, LANES)
    out = jnp.dot(both, table, precision=highest, preferred_element_type=jnp.float32)
    return out.reshape(shape)


def left_and_right(flags, a, b):
    even = flagged(flags, S_EVEN, a.shape)
    return jnp.where(even, b, a), jnp.where(even, a, b)


def widened(flags, own, a, b):
    sub = place_in_segment()
    left, right = left_and_right(flags, a, b)
    x = jnp.where((sub >= 8) & (sub < 16), pltpu.roll(right, LANES - 16, axis=1), own)
    return jnp.where((sub >= 16) & (sub < 24), pltpu.roll(left, 16, axis=1), x)


def widened_other(flags, own, a, b):
    sub = place_in_segment()
    left, right = left_and_right(flags, a, b)
    low = pltpu.roll(jnp.where((sub >= 16) & (sub < 24), right, own), LANES - 8, axis=1)
    high = pltpu.roll(jnp.where((sub >= 8) & (sub < 16), left, own), 8, axis=1)
    return jnp.where(sub < 16, low, high)


def inner_coefficients(flow, cm, tf, lf, ln, shared, radii, at_cell):
    @each(LAYERS, True)
    def _(l):
        u = [flow[k, l] for k in range(FIELDS)]
        p, radius, _, cells = primitives(u)
        for i, x in enumerate(cells):
            cm[i, l] = x
        shared[0, l] = p
        shared[1, l] = radius[0]
        radii[l] = radius[2]
        at_cell(l, radius[0] + radius[1] + radius[2])
        for i, x in enumerate(rolled_faces(u, p, radius[1], 1)):
            tf[i, l] = x

    @each(2, True)
    def _(half):
        rows = half_rows(half)
        cell = [[flow[k, l, rows] for k in range(FIELDS)] for l in range(LAYERS)]
        pressure = [shared[0, l, rows] for l in range(LAYERS)]
        radius = [radii[l, rows] for l in range(LAYERS)]
        nus = {}
        for j in range(-1, LAYERS + 1):
            nu, n0, n1 = sensor_terms(*[pressure[clamp(j + d)] for d in (-1, 0, 1)])
            nus[j] = nu
            ln[0, j + 1, rows] = n0
            ln[1, j + 1, rows] = n1
        for f in range(-1, LAYERS):
            terms = face_terms(
                nus[f],
                nus[f + 1],
                radius[clamp(f)],
                radius[clamp(f + 1)],
                *[cell[clamp(f + d)] for d in (-1, 0, 1, 2)],
            )
            for i, x in enumerate(terms):
                lf[i, f + 1, rows] = x


def outer_coefficients(flags, flow, own, from_a, from_b, zone_a, near, far, maps, shared, ch, cs, xf, ts):
    through = mapped(near[:, 0:16], far[:, 0:16], maps)
    even = flagged(flags, B_EVEN, (16, LANES))
    plane = flagged(flags, PLANE, (16, LANES))
    row = iota((8, LANES), 0)
    inlet = flagged(flags, INLET, (8, LANES))
    outlet = flagged(flags, OUTLET, (8, LANES))
    lower, upper = [], []
    for k in range(FIELDS):
        b = jnp.where(plane, through[k], near[k, 0:16])
        a = zone_a[k, 0:16]
        lower.append(jnp.where(even, b, a))
        upper.append(jnp.where(even, a, b))
    for l in range(LAYERS):
        u, halo = [], []
        for k in range(FIELDS):
            main = flow[k, l]
            up = jnp.where(outlet, jnp.broadcast_to(main[15:16], (8, LANES)), quad(upper[k], l, False))
            low = jnp.where(inlet, jnp.broadcast_to(main[0:1], (8, LANES)), quad(lower[k], l, True))
            halo.append(jnp.where(row < 4, up, low))
            u.append(jnp.concatenate([main, halo[k]], axis=0))
        p, radius, _, cells = primitives(halo)
        for i, x in enumerate(cells):
            ch[i, l] = x
        p = jnp.concatenate([shared[0, l], p], axis=0)
        radius = jnp.concatenate([shared[1, l], radius[0]], axis=0)
        for i, x in enumerate(rolled_faces(u, p, radius, 0)):
            xf[i, l] = x
    u = [widened(flags, own[k], from_a[k, 0:16], from_b[k, 0:16]) for k in range(FIELDS)]
    p, radius, _, cells = primitives(u)
    for i, x in enumerate(cells):
        cs[i] = x
    for i, x in enumerate(rolled_faces(u, p, radius[1], 1)):
        ts[i] = x


def x_terms(flags, psi, halo, coefs, acc, ghost):
    cm, ch, _, xf, _ = coefs
    row = iota((8, LANES), 0)
    inlet = flagged(flags, INLET, (8, LANES)) & (row == 0)
    outlet = flagged(flags, OUTLET, (8, LANES)) & (row == 7)
    for l in range(LAYERS):
        wide = [jnp.concatenate([psi[k, l], halo(k, l)], axis=0) for k in range(FIELDS)]
        cells = [jnp.concatenate([cm[i, l], ch[i, l]], axis=0) for i in range(CELLS)]
        g = rolled_transpose(wide, lambda i: xf[i, l], cells, 0, 0)
        for k in range(FIELDS):
            out = g[k][16:]
            if ghost is not None:
                ghost[k, l] = out
            first = pltpu.roll(out, 2, axis=0) + pltpu.roll(out, 1, axis=0)
            last = pltpu.roll(out, 7, axis=0) + pltpu.roll(out, 6, axis=0)
            acc[k, l, 0:8] = g[k][0:8] + jnp.where(inlet, first, 0.0)
            acc[k, l, 8:16] = g[k][8:16] + jnp.where(outlet, last, 0.0)


def strip_terms(values, edges, coefs, strip):
    _, _, cs, _, ts = coefs
    g = rolled_transpose(values, lambda i: ts[i], [cs[i] for i in range(CELLS)], 1, 1, edges)
    for k in range(FIELDS):
        strip[k] = g[k]


def t_terms(psi, cm, tf, acc, looped):
    lane = iota((ROWS, LANES), 1)
    inner = (lane >= 1) & (lane < LANES - 2)

    @each(LAYERS, looped)
    def _(l):
        g = rolled_transpose(
            [psi[k, l] for k in range(FIELDS)],
            lambda i: tf[i, l],
            [cm[i, l] for i in range(CELLS)],
            1,
            1,
            inner,
        )
        for k in range(FIELDS):
            acc[k, l] = g[k]


def l_terms(psi, cm, lf, ln, acc, looped):
    last = LAYERS - 1

    @each(2, looped)
    def _(half):
        rows = half_rows(half)
        value = [[psi[k, l, rows] for k in range(FIELDS)] for l in range(LAYERS)]
        w, c, gl, ge = {}, {}, {}, {}
        for f in range(-1, LAYERS):
            if f < 0:
                w[f] = [-x for x in value[0]]
            elif f == last:
                w[f] = value[last]
            else:
                w[f] = [x - y for x, y in zip(value[f], value[f + 1])]
            gl[f] = dot5(w[f], [lf[DL + k, f + 1, rows] for k in range(FIELDS)])
            ge[f] = dot5(w[f], [lf[ES + k, f + 1, rows] for k in range(FIELDS)])
            a4 = lf[A4, f + 1, rows]
            c[f] = [a4 * x for x in w[f]]
        z = {}
        for f in range(last):
            a2 = lf[A2, f + 1, rows]
            z[f] = [a2 * w[f][k] + 2.0 * c[f][k] - c[f + 1][k] - c[f - 1][k] for k in range(FIELDS)]
        nbar = [None] * LAYERS
        for j in range(-1, LAYERS + 1):
            nu_bar = ge.get(j, 0.0) + ge.get(j - 1, 0.0)
            here = ln[0, j + 1, rows] * nu_bar
            side = ln[1, j + 1, rows] * nu_bar
            for to, x in ((j, here), (j - 1, side), (j + 1, side)):
                to = clamp(to)
                nbar[to] = x if nbar[to] is None else nbar[to] + x
        for j in range(LAYERS):
            if j == 0:
                s = [0.5 * w[0][k] + w[-1][k] for k in range(FIELDS)]
                lin = z[0]
                rbar = gl[0] + 2.0 * gl[-1]
            elif j == last:
                s = [0.5 * w[last - 1][k] + w[last][k] for k in range(FIELDS)]
                lin = [-x for x in z[last - 1]]
                rbar = gl[last - 1] + 2.0 * gl[last]
            else:
                s = [0.5 * (w[j][k] + w[j - 1][k]) for k in range(FIELDS)]
                lin = [z[j][k] - z[j - 1][k] for k in range(FIELDS)]
                rbar = gl[j] + gl[j - 1]
            g = to_state(lin, s, rbar, nbar[j], [cm[i, j, rows] for i in range(CELLS)], 2)
            for k in range(FIELDS):
                acc[k, j, rows] = acc[k, j, rows] + g[k]


def outer_terms(flags, psi, coefs, acc, strip, to_a, to_b, ghost):
    even = flagged(flags, B_EVEN, (8, LANES))
    empty = jnp.zeros((8, LANES), jnp.float32)
    x_terms(flags, psi, lambda k, l: empty, coefs, acc, ghost)
    for k in range(FIELDS):
        high = packed_rows([ghost[k, l] for l in range(LAYERS)])
        low = packed_rows([pltpu.roll(ghost[k, l], 2, axis=0) for l in range(LAYERS)])
        to_a[k] = jnp.where(even, high, low)
        to_b[k] = jnp.where(even, low, high)
    sub = place_in_segment()
    edges = ((sub >= 6) & (sub < 8)) | ((sub >= 23) & (sub < 25))
    values = [packed_strip([psi[k, l] for l in range(LAYERS)]) for k in range(FIELDS)]
    strip_terms(values, edges, coefs, strip)


def settle(psi, outer, inner, keep, factor, pushed, base, looped):
    @each(LAYERS, looped)
    def _(l):
        for k in range(FIELDS):
            total = inner[k, l] if outer is None else outer[k, l] + inner[k, l]
            base[k, l] = psi[k, l] * keep[l] - factor[l] * total + pushed[k, l]


def arrived_rows(flags, lower, upper):
    row = iota((8, LANES), 0)
    first = (row < 2) & jnp.logical_not(flagged(flags, INLET, (8, LANES)))
    last = (row >= 6) & jnp.logical_not(flagged(flags, OUTLET, (8, LANES)))

    def rows(k, l):
        low = jnp.where(first, pair(lower[k], l, 0), 0.0)
        high = jnp.where(last, pair(upper[k], l, 6), 0.0)
        return jnp.concatenate([low, high], axis=0)

    return rows


def facing_gradients(flags, flow, from_a, from_b, near, far, maps):
    rotor = jnp.logical_not(flagged(flags, B_EVEN, (8, LANES)))
    row = iota((8, LANES), 0)
    panel = []
    for k in range(FIELDS):
        low = packed_rows([flow[k, l, 0:8] for l in range(LAYERS)])
        high = packed_rows([pltpu.roll(flow[k, l, 8:16], 2, axis=0) for l in range(LAYERS)])
        panel.append(jnp.where(rotor, high, low))
    panel = jnp.stack(panel)
    first, second = [], []
    for k in range(FIELDS):
        left, right = left_and_right(flags, from_a[k, 16:24], from_b[k, 16:24])
        first.append(jnp.where(rotor, left, right))
        second.append(jnp.where(rotor, right, left))
    ghosts = (
        mapped(panel, jnp.stack(first), maps),
        mapped(jnp.stack(second), panel, maps),
    )
    kept = (row == 7) | (rotor & (row == 0)) | (jnp.logical_not(rotor) & (row == 6))
    out = []
    for ghost, facing in zip(ghosts, (near, far)):
        layers = []
        for l in range(LAYERS):
            u, psi = [], []
            for k in range(FIELDS):
                cells = facing[k, 0:16]
                below = pair(ghost[k], l, 6)
                above = pair(ghost[k], l, 0)
                as_rotor = jnp.where(
                    row < 4,
                    quad(cells, l, False),
                    jnp.where(row < 6, pltpu.roll(below, 6, axis=0), below),
                )
                as_stator = jnp.where(
                    row < 2,
                    above,
                    jnp.where(row < 4, pltpu.roll(above, 2, axis=0), quad(cells, l, True)),
                )
                u.append(jnp.where(rotor, as_rotor, as_stator))
                value = facing[k, 16:24]
                psi.append(
                    jnp.where(
                        rotor,
                        jnp.where(row < 2, pair(value, l, 0), 0.0),
                        jnp.where(row >= 6, pair(value, l, 6), 0.0),
                    )
                )
            p, radius, _, cells = primitives(u)
            faces = rolled_faces(u, p, radius[0], 0)
            g = rolled_transpose(psi, lambda i: faces[i], cells, 0, 0, kept)
            layers.append([jnp.where(rotor, pltpu.roll(x, 2, axis=0), x) for x in g])
        out.append(jnp.stack([packed_rows([layers[l][k] for l in range(LAYERS)]) for k in range(FIELDS)]))
    return out


def prepare_kernel(
    flags, panel_maps, flow, adjoint, later, gradient, volume,
    state_maps, grad_maps, keep, factor, pushed, own, base, cm, tf, lf, ln, shared, sems, acc, radii,
):
    of_phase = panel_maps.at[flags[PHASE]]
    copies = [
        pltpu.make_async_copy(of_phase.at[pl.ds(flags[which], 2)], to, sems.at[i])
        for i, (which, to) in enumerate(((STATE_MAPS, state_maps), (GRAD_MAPS, grad_maps)))
    ]
    for copy in copies:
        copy.start()

    def at_cell(l, radius_sum):
        vol = volume[l]
        f = courant / (radius_sum + (1.5 * courant / physical_step) * vol)
        factor[l] = f
        keep[l] = 1.0 - f * ((1.5 / physical_step) * vol)
        for k in range(FIELDS):
            source = gradient[k, l] + vol * (2.0 * later[0, k, l] - 0.5 * later[1, k, l]) / physical_step
            pushed[k, l] = f * source

    inner_coefficients(flow, cm, tf, lf, ln, shared, radii, at_cell)

    @each(FIELDS, True)
    def _(k):
        own[k] = packed_edges([flow[k, l] for l in range(LAYERS)], [adjoint[k, l] for l in range(LAYERS)])

    t_terms(adjoint, cm, tf, acc, True)
    l_terms(adjoint, cm, lf, ln, acc, True)
    settle(adjoint, None, acc, keep, factor, pushed, base, True)
    for copy in copies:
        copy.wait()


def start_kernel(
    flags, flow, adjoint, from_a, from_b, zone_a, near, far, state_maps, grad_maps, factor, own, base, cm, shared,
    psi, acc, strip, to_a, to_b, ch, cs, xf, ts, ghost,
):
    coefs = (cm, ch, cs, xf, ts)
    outer_coefficients(flags, flow, own, from_a, from_b, zone_a, near, far, state_maps, shared, ch, cs, xf, ts)
    even = flagged(flags, B_EVEN, (8, LANES))
    plane = flagged(flags, PLANE, (8, LANES))
    row = iota((8, LANES), 0)
    use_upper = (row < 2) & jnp.logical_not(flagged(flags, OUTLET, (8, LANES)))
    use_lower = (row >= 6) & jnp.logical_not(flagged(flags, INLET, (8, LANES)))

    def halo(k, l):
        a = zone_a[k, 16:24]
        b = jnp.where(plane, 0.0, near[k, 16:24])
        upper = pair(jnp.where(even, a, b), l, 0)
        lower = pair(jnp.where(even, b, a), l, 6)
        return jnp.where(use_upper, upper, jnp.where(use_lower, lower, 0.0))

    x_terms(flags, adjoint, halo, coefs, acc, None)
    sub = place_in_segment()
    edges = ((sub >= 6) & (sub < 9)) | ((sub >= 22) & (sub < 25))
    values = [widened_other(flags, own[k], from_a[k, 0:16], from_b[k, 0:16]) for k in range(FIELDS)]
    strip_terms(values, edges, coefs, strip)
    panels = facing_gradients(flags, flow, from_a, from_b, near, far, grad_maps)
    through = mapped_back(panels[0], panels[1], grad_maps)
    lower, upper = [], []
    for k in range(FIELDS):
        b = jnp.where(plane, through[k], 0.0)
        lower.append(jnp.where(even, b, 0.0))
        upper.append(jnp.where(even, 0.0, b))
    rows = arrived_rows(flags, lower, upper)
    for k in range(FIELDS):
        for l in range(LAYERS):
            total = acc[k, l] + from_strip(strip[k], l) + rows(k, l)
            psi[k, l] = base[k, l] - factor[l] * total
    outer_terms(flags, psi, coefs, acc, strip, to_a, to_b, ghost)


def inner_kernel(flags, psi, outer, keep, factor, pushed, cm, tf, lf, ln, base, acc):
    t_terms(psi, cm, tf, acc, False)
    l_terms(psi, cm, lf, ln, acc, False)
    settle(psi, outer, acc, keep, factor, pushed, base, False)


def advance(flags, base, strip, from_a, from_b, zone_a, near, far, maps, factor, out):
    through = mapped_back(near[...], far[...], maps)
    even = flagged(flags, B_EVEN, (8, LANES))
    plane = flagged(flags, PLANE, (8, LANES))
    sub = place_in_segment()
    whole, lower, upper = [], [], []
    for k in range(FIELDS):
        left, right = left_and_right(flags, from_a[k], from_b[k])
        right = jnp.where(sub < 8, pltpu.roll(right, LANES - 16, axis=1), 0.0)
        whole.append(strip[k] + jnp.where(sub >= 24, pltpu.roll(left, 16, axis=1), right))
        b = jnp.where(plane, through[k], near[k])
        a = zone_a[k]
        lower.append(jnp.where(even, b, a))
        upper.append(jnp.where(even, a, b))
    rows = arrived_rows(flags, lower, upper)
    for k in range(FIELDS):
        for l in range(LAYERS):
            out[k, l] = base[k, l] - factor[l] * (from_strip(whole[k], l) + rows(k, l))


def step_kernel(
    flags, base, strip, from_a, from_b, zone_a, near, far, maps, factor, cm, ch, cs, xf, ts,
    psi, acc, strip_out, to_a, to_b, ghost,
):
    advance(flags, base, strip, from_a, from_b, zone_a, near, far, maps, factor, psi)
    outer_terms(flags, psi, (cm, ch, cs, xf, ts), acc, strip_out, to_a, to_b, ghost)


def last_kernel(flags, base, strip, from_a, from_b, zone_a, near, far, maps, factor, out):
    advance(flags, base, strip, from_a, from_b, zone_a, near, far, maps, factor, out)


def f32(*shape):
    return jax.ShapeDtypeStruct(shape, jnp.float32)


STATE = (FIELDS, LAYERS, ROWS, LANES)
STRIP = (FIELDS, ROWS, LANES)
PANEL = (FIELDS, 8, LANES)
SCALAR = (LAYERS, ROWS, LANES)
FIRST = ((FIELDS, 24, LANES),) * 3
MAPS = (2, LANES, LANES)
GHOST = (FIELDS, LAYERS, 8, LANES)
TERMS = (f32(*STATE), f32(*STATE), f32(*STRIP), f32(*PANEL), f32(*PANEL))
FIXED = (f32(*SCALAR), f32(*SCALAR), f32(*STATE))
INNER = (
    f32(CELLS, *SCALAR),
    f32(FACES, *SCALAR),
    f32(12, LAYERS + 1, ROWS, LANES),
    f32(2, LAYERS + 2, ROWS, LANES),
)
SHARED = f32(2, *SCALAR)
OUTER = (
    f32(CELLS, LAYERS, 8, LANES),
    f32(CELLS, ROWS, LANES),
    f32(FACES, LAYERS, ROWS + 8, LANES),
    f32(FACES, ROWS, LANES),
)


def call(kernel, outs, args, work=(), name=None, in_place=None, away=(), copies=0):
    vmem = pl.BlockSpec(memory_space=pltpu.VMEM)
    smem = pl.BlockSpec(memory_space=pltpu.SMEM)
    there = pl.BlockSpec(memory_space=pltpu.HBM)
    return pl.pallas_call(
        kernel,
        out_shape=outs,
        in_specs=[smem] + [there if i in away else vmem for i in range(1, len(args))],
        out_specs=[vmem] * len(outs) if isinstance(outs, tuple) else vmem,
        scratch_shapes=([pltpu.SemaphoreType.DMA((copies,))] if copies else [])
        + [pltpu.VMEM(shape, jnp.float32) for shape in work],
        compiler_params=pltpu.CompilerParams(vmem_limit_bytes=32 * 1024 * 1024),
        input_output_aliases=in_place or {},
        name=name,
    )(*args)


def swaps(names, sectors, blocks, turn):
    half = blocks // 2
    assert half % 2 == 0
    where = {"sector": sectors, "block": blocks}
    minor = where[names[1]]

    def flat(b, s):
        first, second = (s, b) if names[0] == "sector" else (b, s)
        return first * minor + second

    sector_a, sector_b, block_a, near, far = [], [], [], [], []
    for b in range(blocks):
        for s in range(sectors):
            me = flat(b, s)
            sector_a.append((me, flat(b, s ^ 1)))
            sector_b.append((me, flat(b, (s + (1 if s % 2 else -1)) % sectors)))
            block_a.append((me, flat(b ^ 1, s)))
            if b == half - 1:
                near.append((me, flat(half, (s + turn) % sectors)))
                far.append((me, flat(half, (s + turn + 1) % sectors)))
            elif b == half:
                near.append((me, flat(half - 1, (s - turn) % sectors)))
                far.append((me, flat(half - 1, (s - turn - 1) % sectors)))
            else:
                other = b + 1 if b % 2 else b - 1
                near.append((me, flat(other, s) if 0 <= other < blocks else me))
                far.append((me, me))
    return sector_a, sector_b, block_a, near, far


def exchange(names, sectors, blocks, offset, strip, to_a, to_b, beside=None, args=()):
    def branch(shift):
        sector_a, sector_b, block_a, near, far = swaps(names, sectors, blocks, shift)

        def run(strip, to_a, to_b, *args):
            move = lambda x, pairs: lax.ppermute(x, names, pairs)
            moved = (
                move(strip, sector_a),
                move(strip, sector_b),
                move(to_a, block_a),
                move(to_b, near),
                move(to_b, far),
            )
            return moved if beside is None else moved + tuple(beside(*args))

        return run

    return tuple(
        lax.switch(offset, [branch(shift) for shift in range(sectors)], strip, to_a, to_b, *args)
    )


def first_beside(*args):
    return call(
        prepare_kernel,
        (f32(*MAPS), f32(*MAPS)) + FIXED + (f32(*STRIP), f32(*STATE)) + INNER + (SHARED,),
        args,
        (STATE, SCALAR),
        name="prepare",
        away=(1,),
        copies=2,
    )


def next_beside(*args):
    return (call(inner_kernel, f32(*STATE), args, (STATE,), name="inner", in_place={2: 0}),)


def shards(flow, adjoint, adjoint_later, objective_grad, volume, panel_maps, rotor_step, names):
    blocks = lax.axis_size("block")
    sectors = lax.axis_size("sector")
    place = lax.axis_index("block")
    half = blocks // 2
    stator = place >= half
    turn = rotor_step[0]
    offset = (turn // PHASES) % sectors
    flags = jnp.stack(
        [
            (lax.axis_index("sector") % 2 == 0).astype(jnp.int32),
            (place % 2 == 0).astype(jnp.int32),
            (place == 0).astype(jnp.int32),
            (place == blocks - 1).astype(jnp.int32),
            ((place == half) | (place == half - 1)).astype(jnp.int32),
            turn % PHASES,
            jnp.where(stator, 0, 2).astype(jnp.int32),
            jnp.where(stator, 2, 0).astype(jnp.int32),
        ]
    )
    send = partial(exchange, names, sectors, blocks, offset)
    packed = tuple(
        call(
            pack_kernel,
            tuple(f32(*shape) for shape in FIRST),
            (flags, flow, adjoint),
            name="pack",
        )
    )
    arrived = send(
        *packed,
        beside=first_beside,
        args=(
            flags,
            panel_maps,
            flow,
            adjoint,
            adjoint_later,
            objective_grad,
            volume,
        ),
    )
    (state_maps, maps, keep, factor, pushed, own, base), inner, shared = arrived[5:12], arrived[12:16], arrived[16]
    cm = inner[0]
    out = call(
        start_kernel,
        TERMS + OUTER,
        (flags, flow, adjoint) + arrived[:5] + (state_maps, maps, factor, own, base, cm, shared),
        (GHOST,),
        name="start",
    )
    terms, outer = tuple(out[:5]), tuple(out[5:])
    for sweep in range(1, ITERS):
        psi, acc, strip, to_a, to_b = terms
        arrived = send(
            strip, to_a, to_b, beside=next_beside, args=(flags, psi, acc, keep, factor, pushed) + inner
        )
        args = (flags, arrived[5], strip) + arrived[:5] + (maps, factor)
        if sweep == ITERS - 1:
            return call(last_kernel, f32(*STATE), args, name="last")
        terms = tuple(call(step_kernel, TERMS, args + (cm,) + outer, (GHOST,), name="step"))


def solution(mesh):
    placed = (
        P(None, None, "block", "sector"),
        P(None, None, "block", "sector"),
        P(None, None, None, "block", "sector"),
        P(None, None, "block", "sector"),
        P(None, "block", "sector"),
        P(),
        P(),
    )
    return jax.shard_map(
        partial(shards, names=tuple(mesh.axis_names)),
        mesh=mesh,
        in_specs=placed,
        out_specs=P(None, None, "block", "sector"),
        check_vma=False,
    )
```

profile of v0, /device:TPU:9, one launch (start us, length us, event | category | flops | bytes accessed | tf_op | source)
XLA Modules:
  0.0 59.7 jit_solution(17808821595756587523)
XLA Ops:
  0.8 0.1 copy-done.1
  0.9 1.1 %pack.1 = (f32[5,24,128]{2,1,0:T(8,128)S(1)}, f32[5,24,128]{2,1,0:T(8,128)S(1)}, f32[5,24,128]{2,1,0:T(8,128)S(1)}) custom-call(s32[8]{0:T(128)S(1)} %stack.55.flags, f32[5,4,16,128]{3,2,1,0:T(8,128)S(1)} %copy-done.1, f32[5,4,16,128]{3,2,1,0:T(8,128)} %adjoint.1), custom_call_target="tpu_custom_call" | custom-call | tf_op jit(solution)/shard_map/pack/pallas_call | solution.py:679
  2.1 14.4 %conditional.4 = (f32[5,24,128]{2,1,0:T(8,128)}, f32[5,24,128]{2,1,0:T(8,128)}, f32[5,24,128]{2,1,0:T(8,128)}, f32[5,24,128]{2,1,0:T(8,128)}, f32[5,24,128]{2,1,...) conditional(s32[]{:T(128)} %clamp.2, ...), branch_computations={%region_0.1_spmd, %region_1.2_spmd, %region_2.3_spmd, %region_3.4_... | conditional | bytes 1229136 | solution.py:740
  2.2 2.2 %collective-permute-start.21 = (f32[5,24,128]{2,1,0:T(8,128)S(1)}, f32[5,24,128]{2,1,0:T(8,128)}, u32[]{:S(2)}, u32[]{:S(2)}) collective-permute-start(f32[5,24,128]{2,1,0:T(8,128)S(1)} %get-tuple-element.877), channel_id=1, source_target_pairs={{0,28},{4,8},{8,4},{12,16},{16,12},{20,24},{24,20},{28,0},{1,29},{... | collective-permute-start | bytes 184328 | tf_op jit(solution)/shard_map/cond/branch_4_fun/ppermute | solution.py:727
  4.4 0.5 collective-permute-start.20
  4.9 5.1 %collective-permute-start.24 = (f32[5,24,128]{2,1,0:T(8,128)S(1)}, f32[5,24,128]{2,1,0:T(8,128)}, u32[]{:S(2)}, u32[]{:S(2)}) collective-permute-start(f32[5,24,128]{2,1,0:T(8,128)S(1)} %get-tuple-element.879), channel_id=1, source_target_pairs={{0,0},{4,4},{8,8},{12,12},{16,16},{20,20},{24,24},{28,28},{1,22},{... | collective-permute-start | bytes 184328 | tf_op jit(solution)/shard_map/cond/branch_4_fun/ppermute | solution.py:727
  10.0 1.9 %collective-permute-start.23 = (f32[5,24,128]{2,1,0:T(8,128)S(1)}, f32[5,24,128]{2,1,0:T(8,128)}, u32[]{:S(2)}, u32[]{:S(2)}) collective-permute-start(f32[5,24,128]{2,1,0:T(8,128)S(1)} %get-tuple-element.879), channel_id=1, source_target_pairs={{0,0},{4,4},{8,8},{12,12},{16,16},{20,20},{24,24},{28,28},{1,18},{... | collective-permute-start | bytes 184328 | tf_op jit(solution)/shard_map/cond/branch_4_fun/ppermute | solution.py:727
  11.9 3.8 %prepare.12 = (f32[2,128,128]{2,1,0:T(8,128)S(1)}, f32[2,128,128]{2,1,0:T(8,128)S(1)}, f32[4,16,128]{2,1,0:T(8,128)S(1)}, f32[4,16,128]{2,1,0:T(8,128)S(1)}, f32...) custom-call(s32[8]{0:T(128)S(1)} %get-tuple-element.880.flags, ...), custom_call_target="tpu_custom_call" | custom-call | tf_op jit(solution)/shard_map/cond/branch_4_fun/prepare/pallas_call | solution.py:679
  15.7 0.7 %collective-permute-done.23 = f32[5,24,128]{2,1,0:T(8,128)} collective-permute-done((f32[5,24,128]{2,1,0:T(8,128)S(1)}, f32[5,24,128]{2,1,0:T(8,128)}, u32[]{:S(2)}, u32[]{:S(2)}) %collective-permute-start.23) | collective-permute-done | bytes 61472 | tf_op jit(solution)/shard_map/cond/branch_4_fun/ppermute | solution.py:727
  16.4 3.4 %start.1 = (f32[5,4,16,128]{3,2,1,0:T(8,128)S(1)}, f32[5,4,16,128]{3,2,1,0:T(8,128)S(1)}, f32[5,16,128]{2,1,0:T(8,128)S(1)}, f32[5,8,128]{2,1,0:T(8,128)S(1)}, f...) custom-call(s32[8]{0:T(128)S(1)} %stack.55.flags, ...), custom_call_target="tpu_custom_call" | custom-call | tf_op jit(solution)/shard_map/start/pallas_call | solution.py:679
  19.9 11.7 %conditional.5 = (f32[5,16,128]{2,1,0:T(8,128)}, f32[5,16,128]{2,1,0:T(8,128)}, f32[5,8,128]{2,1,0:T(8,128)}, f32[5,8,128]{2,1,0:T(8,128)}, f32[5,8,128]{2,1,0:T(8,128)}, /*index=5*/f32[5,4,16,128]{3,2,1,0:T(8,128)S(1)}) conditional(s32[]{:T(128)} %clamp.2, (f32[5,16,128]{2,1,0:T(8,128)S(1)}, ...), branch_computations={%region_8.9_spmd, %region_9.10_spmd, %region_10.11_spmd, %region_1... | conditional | bytes 573688 | solution.py:740
  20.1 1.1 %collective-permute-start.61 = (f32[5,16,128]{2,1,0:T(8,128)S(1)}, f32[5,16,128]{2,1,0:T(8,128)}, u32[]{:S(2)}, u32[]{:S(2)}) collective-permute-start(f32[5,16,128]{2,1,0:T(8,128)S(1)} %get-tuple-element.1017), channel_id=1, source_target_pairs={{0,28},{4,8},{8,4},{12,16},{16,12},{20,24},{24,20},{28,0},{1,29},{... | collective-permute-start | bytes 122888 | tf_op jit(solution)/shard_map/cond/branch_4_fun/ppermute | solution.py:727
  21.2 0.7 %collective-permute-start.60 = (f32[5,16,128]{2,1,0:T(8,128)S(1)}, f32[5,16,128]{2,1,0:T(8,128)}, u32[]{:S(2)}, u32[]{:S(2)}) collective-permute-start(f32[5,16,128]{2,1,0:T(8,128)S(1)} %get-tuple-element.1017), channel_id=1, source_target_pairs={{0,4},{4,0},{8,12},{12,8},{16,20},{20,16},{24,28},{28,24},{1,5},{5... | collective-permute-start | bytes 122888 | tf_op jit(solution)/shard_map/cond/branch_4_fun/ppermute | solution.py:727
  21.9 4.1 %collective-permute-start.64 = (f32[5,8,128]{2,1,0:T(8,128)S(1)}, f32[5,8,128]{2,1,0:T(8,128)}, u32[]{:S(2)}, u32[]{:S(2)}) collective-permute-start(f32[5,8,128]{2,1,0:T(8,128)S(1)} %get-tuple-element.1019), channel_id=1, source_target_pairs={{0,0},{4,4},{8,8},{12,12},{16,16},{20,20},{24,24},{28,28},{1,22},{... | collective-permute-start | bytes 61448 | tf_op jit(solution)/shard_map/cond/branch_4_fun/ppermute | solution.py:727
  26.0 2.0 %collective-permute-start.63 = (f32[5,8,128]{2,1,0:T(8,128)S(1)}, f32[5,8,128]{2,1,0:T(8,128)}, u32[]{:S(2)}, u32[]{:S(2)}) collective-permute-start(f32[5,8,128]{2,1,0:T(8,128)S(1)} %get-tuple-element.1019), channel_id=1, source_target_pairs={{0,0},{4,4},{8,8},{12,12},{16,16},{20,20},{24,24},{28,28},{1,18},{... | collective-permute-start | bytes 61448 | tf_op jit(solution)/shard_map/cond/branch_4_fun/ppermute | solution.py:727
  28.0 1.1 %inner.28 = f32[5,4,16,128]{3,2,1,0:T(8,128)S(1)} custom-call(s32[8]{0:T(128)S(1)} %get-tuple-element.1020.flags, f32[5,4,16,128]{3,2,1,0:T(8,128)S(1)} %get-tuple-element.1021.psi, f32[5,4,16,128]{3,2,1,0:T(8,128)S(1)} %get-tuple-element.1022.outer, f32[4,16,128]{2,1,0:T(8,128)S(1)} %get-tuple-element.1023.keep, ...), custom_call_target="tpu_custom_call", output_to_operand_aliasing={{}: (2, {})} | custom-call | tf_op jit(solution)/shard_map/cond/branch_4_fun/inner/pallas_call | solution.py:679
  29.1 2.4 %collective-permute-done.63 = f32[5,8,128]{2,1,0:T(8,128)} collective-permute-done((f32[5,8,128]{2,1,0:T(8,128)S(1)}, f32[5,8,128]{2,1,0:T(8,128)}, u32[]{:S(2)}, u32[]{:S(2)}) %collective-permute-start.63) | collective-permute-done | bytes 20512 | tf_op jit(solution)/shard_map/cond/branch_4_fun/ppermute | solution.py:727
  31.5 1.8 %step.2 = (f32[5,4,16,128]{3,2,1,0:T(8,128)S(1)}, f32[5,4,16,128]{3,2,1,0:T(8,128)S(1)}, f32[5,16,128]{2,1,0:T(8,128)S(1)}, f32[5,8,128]{2,1,0:T(8,128)S(1)}, f32[5,8,128]{2,1,0:T(8,128)S(1)}) custom-call(s32[8]{0:T(128)S(1)} %stack.55.flags, f32[5,4,16,128]{3,2,1,0:T(8,128)S(1)} %get-tuple-element.1359.base, f32[5,16,128]{2,1,0:T(8,128)S(1)} %get-tuple-element.1349.strip, ...), custom_call_target="tpu_custom_call" | custom-call | tf_op jit(solution)/shard_map/step/pallas_call | solution.py:679
  33.3 11.8 %conditional.6 = (f32[5,16,128]{2,1,0:T(8,128)}, f32[5,16,128]{2,1,0:T(8,128)}, f32[5,8,128]{2,1,0:T(8,128)}, f32[5,8,128]{2,1,0:T(8,128)}, f32[5,8,128]{2,1,0:T(8,128)}, /*index=5*/f32[5,4,16,128]{3,2,1,0:T(8,128)S(1)}) conditional(s32[]{:T(128)} %clamp.2, (f32[5,16,128]{2,1,0:T(8,128)S(1)}, ...), branch_computations={%region_16.17_spmd, %region_17.18_spmd, %region_18.19_spmd, %regio... | conditional | bytes 573688 | solution.py:740
  33.3 1.4 %collective-permute-start.101 = (f32[5,16,128]{2,1,0:T(8,128)S(1)}, f32[5,16,128]{2,1,0:T(8,128)}, u32[]{:S(2)}, u32[]{:S(2)}) collective-permute-start(f32[5,16,128]{2,1,0:T(8,128)S(1)} %get-tuple-element.1121), channel_id=1, source_target_pairs={{0,28},{4,8},{8,4},{12,16},{16,12},{20,24},{24,20},{28,0},{1,29},{... | collective-permute-start | bytes 122888 | tf_op jit(solution)/shard_map/cond/branch_4_fun/ppermute | solution.py:727
  34.7 4.9 %collective-permute-start.104 = (f32[5,8,128]{2,1,0:T(8,128)S(1)}, f32[5,8,128]{2,1,0:T(8,128)}, u32[]{:S(2)}, u32[]{:S(2)}) collective-permute-start(f32[5,8,128]{2,1,0:T(8,128)S(1)} %get-tuple-element.1123), channel_id=1, source_target_pairs={{0,0},{4,4},{8,8},{12,12},{16,16},{20,20},{24,24},{28,28},{1,22},{... | collective-permute-start | bytes 61448 | tf_op jit(solution)/shard_map/cond/branch_4_fun/ppermute | solution.py:727
  39.6 1.9 %collective-permute-start.103 = (f32[5,8,128]{2,1,0:T(8,128)S(1)}, f32[5,8,128]{2,1,0:T(8,128)}, u32[]{:S(2)}, u32[]{:S(2)}) collective-permute-start(f32[5,8,128]{2,1,0:T(8,128)S(1)} %get-tuple-element.1123), channel_id=1, source_target_pairs={{0,0},{4,4},{8,8},{12,12},{16,16},{20,20},{24,24},{28,28},{1,18},{... | collective-permute-start | bytes 61448 | tf_op jit(solution)/shard_map/cond/branch_4_fun/ppermute | solution.py:727
  41.5 1.1 %inner.36 = f32[5,4,16,128]{3,2,1,0:T(8,128)S(1)} custom-call(s32[8]{0:T(128)S(1)} %get-tuple-element.1124.flags, f32[5,4,16,128]{3,2,1,0:T(8,128)S(1)} %get-tuple-element.1125.psi, f32[5,4,16,128]{3,2,1,0:T(8,128)S(1)} %get-tuple-element.1126.outer, f32[4,16,128]{2,1,0:T(8,128)S(1)} %get-tuple-element.1127.keep, ...), custom_call_target="tpu_custom_call", output_to_operand_aliasing={{}: (2, {})} | custom-call | tf_op jit(solution)/shard_map/cond/branch_4_fun/inner/pallas_call | solution.py:679
  42.7 2.4 %collective-permute-done.103 = f32[5,8,128]{2,1,0:T(8,128)} collective-permute-done((f32[5,8,128]{2,1,0:T(8,128)S(1)}, f32[5,8,128]{2,1,0:T(8,128)}, u32[]{:S(2)}, u32[]{:S(2)}) %collective-permute-start.103) | collective-permute-done | bytes 20512 | tf_op jit(solution)/shard_map/cond/branch_4_fun/ppermute | solution.py:727
  45.1 1.8 %step.3 = (f32[5,4,16,128]{3,2,1,0:T(8,128)S(1)}, f32[5,4,16,128]{3,2,1,0:T(8,128)S(1)}, f32[5,16,128]{2,1,0:T(8,128)S(1)}, f32[5,8,128]{2,1,0:T(8,128)S(1)}, f32[5,8,128]{2,1,0:T(8,128)S(1)}) custom-call(s32[8]{0:T(128)S(1)} %stack.55.flags, f32[5,4,16,128]{3,2,1,0:T(8,128)S(1)} %get-tuple-element.1374.base, f32[5,16,128]{2,1,0:T(8,128)S(1)} %get-tuple-element.1369.strip, ...), custom_call_target="tpu_custom_call" | custom-call | tf_op jit(solution)/shard_map/step/pallas_call | solution.py:679
  46.9 11.0 %conditional.7 = (f32[5,16,128]{2,1,0:T(8,128)}, f32[5,16,128]{2,1,0:T(8,128)}, f32[5,8,128]{2,1,0:T(8,128)}, f32[5,8,128]{2,1,0:T(8,128)}, f32[5,8,128]{2,1,0:T(8,128)}, /*index=5*/f32[5,4,16,128]{3,2,1,0:T(8,128)S(1)}) conditional(s32[]{:T(128)} %clamp.2, (f32[5,16,128]{2,1,0:T(8,128)S(1)}, ...), branch_computations={%region_24.25_spmd, %region_25.26_spmd, %region_26.27_spmd, %regio... | conditional | bytes 573688 | solution.py:740
  47.2 1.4 %collective-permute-start.141 = (f32[5,16,128]{2,1,0:T(8,128)S(1)}, f32[5,16,128]{2,1,0:T(8,128)}, u32[]{:S(2)}, u32[]{:S(2)}) collective-permute-start(f32[5,16,128]{2,1,0:T(8,128)S(1)} %get-tuple-element.1225), channel_id=1, source_target_pairs={{0,28},{4,8},{8,4},{12,16},{16,12},{20,24},{24,20},{28,0},{1,29},{... | collective-permute-start | bytes 122888 | tf_op jit(solution)/shard_map/cond/branch_4_fun/ppermute | solution.py:727
  48.6 3.6 %collective-permute-start.144 = (f32[5,8,128]{2,1,0:T(8,128)S(1)}, f32[5,8,128]{2,1,0:T(8,128)}, u32[]{:S(2)}, u32[]{:S(2)}) collective-permute-start(f32[5,8,128]{2,1,0:T(8,128)S(1)} %get-tuple-element.1227), channel_id=1, source_target_pairs={{0,0},{4,4},{8,8},{12,12},{16,16},{20,20},{24,24},{28,28},{1,22},{... | collective-permute-start | bytes 61448 | tf_op jit(solution)/shard_map/cond/branch_4_fun/ppermute | solution.py:727
  52.2 3.0 %collective-permute-start.143 = (f32[5,8,128]{2,1,0:T(8,128)S(1)}, f32[5,8,128]{2,1,0:T(8,128)}, u32[]{:S(2)}, u32[]{:S(2)}) collective-permute-start(f32[5,8,128]{2,1,0:T(8,128)S(1)} %get-tuple-element.1227), channel_id=1, source_target_pairs={{0,0},{4,4},{8,8},{12,12},{16,16},{20,20},{24,24},{28,28},{1,18},{... | collective-permute-start | bytes 61448 | tf_op jit(solution)/shard_map/cond/branch_4_fun/ppermute | solution.py:727
  55.1 1.1 %inner.44 = f32[5,4,16,128]{3,2,1,0:T(8,128)S(1)} custom-call(s32[8]{0:T(128)S(1)} %get-tuple-element.1228.flags, f32[5,4,16,128]{3,2,1,0:T(8,128)S(1)} %get-tuple-element.1229.psi, f32[5,4,16,128]{3,2,1,0:T(8,128)S(1)} %get-tuple-element.1230.outer, f32[4,16,128]{2,1,0:T(8,128)S(1)} %get-tuple-element.1231.keep, ...), custom_call_target="tpu_custom_call", output_to_operand_aliasing={{}: (2, {})} | custom-call | tf_op jit(solution)/shard_map/cond/branch_4_fun/inner/pallas_call | solution.py:679
  56.3 1.7 %collective-permute-done.143 = f32[5,8,128]{2,1,0:T(8,128)} collective-permute-done((f32[5,8,128]{2,1,0:T(8,128)S(1)}, f32[5,8,128]{2,1,0:T(8,128)}, u32[]{:S(2)}, u32[]{:S(2)}) %collective-permute-start.143) | collective-permute-done | bytes 20512 | tf_op jit(solution)/shard_map/cond/branch_4_fun/ppermute | solution.py:727
  58.0 1.7 %last.1 = f32[5,4,16,128]{3,2,1,0:T(8,128)} custom-call(s32[8]{0:T(128)S(1)} %stack.55.flags, f32[5,4,16,128]{3,2,1,0:T(8,128)S(1)} %get-tuple-element.1385.base, f32[5,16,128]{2,1,0:T(8,128)S(1)} %get-tuple-element.1380.strip, f32[5,16,128]{2,1,0:T(8,128)} %get-tuple-element.1386.from_a, f32[5,16,128]{2,1,0:T(8,128)} %get-tuple-element.1387.from_b, ...), custom_call_target="tpu_custom_call" | custom-call | tf_op jit(solution)/shard_map/last/pallas_call | solution.py:679
  (26 shorter events, 0.2 us)
Async XLA Ops:
  0.0 0.9 %copy-start.1 = (f32[5,4,16,128]{3,2,1,0:T(8,128)S(1)}, f32[5,4,16,128]{3,2,1,0:T(8,128)}, u32[]{:S(2)}) copy-start(f32[5,4,16,128]{3,2,1,0:T(8,128)} %flow.3) | copy-start | bytes 491524
  0.0 2.1 %copy-start = (f32[2,5,4,16,128]{4,3,2,1,0:T(8,128)S(1)}, f32[2,5,4,16,128]{4,3,2,1,0:T(8,128)}, u32[]{:S(2)}) copy-start(f32[2,5,4,16,128]{4,3,2,1,0:T(8,128)} %param.41) | copy-start | bytes 983044
  2.1 13.6 %collective-permute-start.22 = (f32[5,24,128]{2,1,0:T(8,128)S(1)}, f32[5,24,128]{2,1,0:T(8,128)}, u32[]{:S(2)}, u32[]{:S(2)}) collective-permute-start(f32[5,24,128]{2,1,0:T(8,128)S(1)} %get-tuple-element.878), channel_id=1, source_target_pairs={{0,1},{4,5},{8,9},{12,13},{16,17},{20,21},{24,25},{28,29},{1,0},{5... | collective-permute-start | bytes 184328 | tf_op jit(solution)/shard_map/cond/branch_4_fun/ppermute | solution.py:727
  2.2 13.5 %collective-permute-start.21 = (f32[5,24,128]{2,1,0:T(8,128)S(1)}, f32[5,24,128]{2,1,0:T(8,128)}, u32[]{:S(2)}, u32[]{:S(2)}) collective-permute-start(f32[5,24,128]{2,1,0:T(8,128)S(1)} %get-tuple-element.877), channel_id=1, source_target_pairs={{0,28},{4,8},{8,4},{12,16},{16,12},{20,24},{24,20},{28,0},{1,29},{... | collective-permute-start | bytes 184328 | tf_op jit(solution)/shard_map/cond/branch_4_fun/ppermute | solution.py:727
  4.4 11.3 %collective-permute-start.20 = (f32[5,24,128]{2,1,0:T(8,128)S(1)}, f32[5,24,128]{2,1,0:T(8,128)}, u32[]{:S(2)}, u32[]{:S(2)}) collective-permute-start(f32[5,24,128]{2,1,0:T(8,128)S(1)} %get-tuple-element.877), channel_id=1, source_target_pairs={{0,4},{4,0},{8,12},{12,8},{16,20},{20,16},{24,28},{28,24},{1,5},{5... | collective-permute-start | bytes 184328 | tf_op jit(solution)/shard_map/cond/branch_4_fun/ppermute | solution.py:727
  4.9 10.8 %collective-permute-start.24 = (f32[5,24,128]{2,1,0:T(8,128)S(1)}, f32[5,24,128]{2,1,0:T(8,128)}, u32[]{:S(2)}, u32[]{:S(2)}) collective-permute-start(f32[5,24,128]{2,1,0:T(8,128)S(1)} %get-tuple-element.879), channel_id=1, source_target_pairs={{0,0},{4,4},{8,8},{12,12},{16,16},{20,20},{24,24},{28,28},{1,22},{... | collective-permute-start | bytes 184328 | tf_op jit(solution)/shard_map/cond/branch_4_fun/ppermute | solution.py:727
  10.0 6.5 %collective-permute-start.23 = (f32[5,24,128]{2,1,0:T(8,128)S(1)}, f32[5,24,128]{2,1,0:T(8,128)}, u32[]{:S(2)}, u32[]{:S(2)}) collective-permute-start(f32[5,24,128]{2,1,0:T(8,128)S(1)} %get-tuple-element.879), channel_id=1, source_target_pairs={{0,0},{4,4},{8,8},{12,12},{16,16},{20,20},{24,24},{28,28},{1,18},{... | collective-permute-start | bytes 184328 | tf_op jit(solution)/shard_map/cond/branch_4_fun/ppermute | solution.py:727
  20.1 11.5 %collective-permute-start.61 = (f32[5,16,128]{2,1,0:T(8,128)S(1)}, f32[5,16,128]{2,1,0:T(8,128)}, u32[]{:S(2)}, u32[]{:S(2)}) collective-permute-start(f32[5,16,128]{2,1,0:T(8,128)S(1)} %get-tuple-element.1017), channel_id=1, source_target_pairs={{0,28},{4,8},{8,4},{12,16},{16,12},{20,24},{24,20},{28,0},{1,29},{... | collective-permute-start | bytes 122888 | tf_op jit(solution)/shard_map/cond/branch_4_fun/ppermute | solution.py:727
  21.2 10.3 %collective-permute-start.60 = (f32[5,16,128]{2,1,0:T(8,128)S(1)}, f32[5,16,128]{2,1,0:T(8,128)}, u32[]{:S(2)}, u32[]{:S(2)}) collective-permute-start(f32[5,16,128]{2,1,0:T(8,128)S(1)} %get-tuple-element.1017), channel_id=1, source_target_pairs={{0,4},{4,0},{8,12},{12,8},{16,20},{20,16},{24,28},{28,24},{1,5},{5... | collective-permute-start | bytes 122888 | tf_op jit(solution)/shard_map/cond/branch_4_fun/ppermute | solution.py:727
  21.9 7.2 %collective-permute-start.62 = (f32[5,8,128]{2,1,0:T(8,128)S(1)}, f32[5,8,128]{2,1,0:T(8,128)}, u32[]{:S(2)}, u32[]{:S(2)}) collective-permute-start(f32[5,8,128]{2,1,0:T(8,128)S(1)} %get-tuple-element.1018), channel_id=1, source_target_pairs={{0,1},{4,5},{8,9},{12,13},{16,17},{20,21},{24,25},{28,29},{1,0},{5... | collective-permute-start | bytes 61448 | tf_op jit(solution)/shard_map/cond/branch_4_fun/ppermute | solution.py:727
  21.9 7.2 %collective-permute-start.64 = (f32[5,8,128]{2,1,0:T(8,128)S(1)}, f32[5,8,128]{2,1,0:T(8,128)}, u32[]{:S(2)}, u32[]{:S(2)}) collective-permute-start(f32[5,8,128]{2,1,0:T(8,128)S(1)} %get-tuple-element.1019), channel_id=1, source_target_pairs={{0,0},{4,4},{8,8},{12,12},{16,16},{20,20},{24,24},{28,28},{1,22},{... | collective-permute-start | bytes 61448 | tf_op jit(solution)/shard_map/cond/branch_4_fun/ppermute | solution.py:727
  26.0 5.5 %collective-permute-start.63 = (f32[5,8,128]{2,1,0:T(8,128)S(1)}, f32[5,8,128]{2,1,0:T(8,128)}, u32[]{:S(2)}, u32[]{:S(2)}) collective-permute-start(f32[5,8,128]{2,1,0:T(8,128)S(1)} %get-tuple-element.1019), channel_id=1, source_target_pairs={{0,0},{4,4},{8,8},{12,12},{16,16},{20,20},{24,24},{28,28},{1,18},{... | collective-permute-start | bytes 61448 | tf_op jit(solution)/shard_map/cond/branch_4_fun/ppermute | solution.py:727
  33.3 11.8 %collective-permute-start.101 = (f32[5,16,128]{2,1,0:T(8,128)S(1)}, f32[5,16,128]{2,1,0:T(8,128)}, u32[]{:S(2)}, u32[]{:S(2)}) collective-permute-start(f32[5,16,128]{2,1,0:T(8,128)S(1)} %get-tuple-element.1121), channel_id=1, source_target_pairs={{0,28},{4,8},{8,4},{12,16},{16,12},{20,24},{24,20},{28,0},{1,29},{... | collective-permute-start | bytes 122888 | tf_op jit(solution)/shard_map/cond/branch_4_fun/ppermute | solution.py:727
  34.7 10.4 %collective-permute-start.100 = (f32[5,16,128]{2,1,0:T(8,128)S(1)}, f32[5,16,128]{2,1,0:T(8,128)}, u32[]{:S(2)}, u32[]{:S(2)}) collective-permute-start(f32[5,16,128]{2,1,0:T(8,128)S(1)} %get-tuple-element.1121), channel_id=1, source_target_pairs={{0,4},{4,0},{8,12},{12,8},{16,20},{20,16},{24,28},{28,24},{1,5},{5... | collective-permute-start | bytes 122888 | tf_op jit(solution)/shard_map/cond/branch_4_fun/ppermute | solution.py:727
  34.7 8.0 %collective-permute-start.102 = (f32[5,8,128]{2,1,0:T(8,128)S(1)}, f32[5,8,128]{2,1,0:T(8,128)}, u32[]{:S(2)}, u32[]{:S(2)}) collective-permute-start(f32[5,8,128]{2,1,0:T(8,128)S(1)} %get-tuple-element.1122), channel_id=1, source_target_pairs={{0,1},{4,5},{8,9},{12,13},{16,17},{20,21},{24,25},{28,29},{1,0},{5... | collective-permute-start | bytes 61448 | tf_op jit(solution)/shard_map/cond/branch_4_fun/ppermute | solution.py:727
  34.7 8.0 %collective-permute-start.104 = (f32[5,8,128]{2,1,0:T(8,128)S(1)}, f32[5,8,128]{2,1,0:T(8,128)}, u32[]{:S(2)}, u32[]{:S(2)}) collective-permute-start(f32[5,8,128]{2,1,0:T(8,128)S(1)} %get-tuple-element.1123), channel_id=1, source_target_pairs={{0,0},{4,4},{8,8},{12,12},{16,16},{20,20},{24,24},{28,28},{1,22},{... | collective-permute-start | bytes 61448 | tf_op jit(solution)/shard_map/cond/branch_4_fun/ppermute | solution.py:727
  39.6 5.5 %collective-permute-start.103 = (f32[5,8,128]{2,1,0:T(8,128)S(1)}, f32[5,8,128]{2,1,0:T(8,128)}, u32[]{:S(2)}, u32[]{:S(2)}) collective-permute-start(f32[5,8,128]{2,1,0:T(8,128)S(1)} %get-tuple-element.1123), channel_id=1, source_target_pairs={{0,0},{4,4},{8,8},{12,12},{16,16},{20,20},{24,24},{28,28},{1,18},{... | collective-permute-start | bytes 61448 | tf_op jit(solution)/shard_map/cond/branch_4_fun/ppermute | solution.py:727
  47.2 10.8 %collective-permute-start.141 = (f32[5,16,128]{2,1,0:T(8,128)S(1)}, f32[5,16,128]{2,1,0:T(8,128)}, u32[]{:S(2)}, u32[]{:S(2)}) collective-permute-start(f32[5,16,128]{2,1,0:T(8,128)S(1)} %get-tuple-element.1225), channel_id=1, source_target_pairs={{0,28},{4,8},{8,4},{12,16},{16,12},{20,24},{24,20},{28,0},{1,29},{... | collective-permute-start | bytes 122888 | tf_op jit(solution)/shard_map/cond/branch_4_fun/ppermute | solution.py:727
  48.6 9.4 %collective-permute-start.140 = (f32[5,16,128]{2,1,0:T(8,128)S(1)}, f32[5,16,128]{2,1,0:T(8,128)}, u32[]{:S(2)}, u32[]{:S(2)}) collective-permute-start(f32[5,16,128]{2,1,0:T(8,128)S(1)} %get-tuple-element.1225), channel_id=1, source_target_pairs={{0,4},{4,0},{8,12},{12,8},{16,20},{20,16},{24,28},{28,24},{1,5},{5... | collective-permute-start | bytes 122888 | tf_op jit(solution)/shard_map/cond/branch_4_fun/ppermute | solution.py:727
  48.6 7.7 %collective-permute-start.142 = (f32[5,8,128]{2,1,0:T(8,128)S(1)}, f32[5,8,128]{2,1,0:T(8,128)}, u32[]{:S(2)}, u32[]{:S(2)}) collective-permute-start(f32[5,8,128]{2,1,0:T(8,128)S(1)} %get-tuple-element.1226), channel_id=1, source_target_pairs={{0,1},{4,5},{8,9},{12,13},{16,17},{20,21},{24,25},{28,29},{1,0},{5... | collective-permute-start | bytes 61448 | tf_op jit(solution)/shard_map/cond/branch_4_fun/ppermute | solution.py:727
  48.6 7.7 %collective-permute-start.144 = (f32[5,8,128]{2,1,0:T(8,128)S(1)}, f32[5,8,128]{2,1,0:T(8,128)}, u32[]{:S(2)}, u32[]{:S(2)}) collective-permute-start(f32[5,8,128]{2,1,0:T(8,128)S(1)} %get-tuple-element.1227), channel_id=1, source_target_pairs={{0,0},{4,4},{8,8},{12,12},{16,16},{20,20},{24,24},{28,28},{1,22},{... | collective-permute-start | bytes 61448 | tf_op jit(solution)/shard_map/cond/branch_4_fun/ppermute | solution.py:727
  52.2 5.8 %collective-permute-start.143 = (f32[5,8,128]{2,1,0:T(8,128)S(1)}, f32[5,8,128]{2,1,0:T(8,128)}, u32[]{:S(2)}, u32[]{:S(2)}) collective-permute-start(f32[5,8,128]{2,1,0:T(8,128)S(1)} %get-tuple-element.1227), channel_id=1, source_target_pairs={{0,0},{4,4},{8,8},{12,12},{16,16},{20,20},{24,24},{28,28},{1,18},{... | collective-permute-start | bytes 61448 | tf_op jit(solution)/shard_map/cond/branch_4_fun/ppermute | solution.py:727
where the time goes:
time: 60.9 us; the launch traced here: 59.7 us
  starting transfers between devices  33.8 us (56%)
  Pallas kernels  17 us (28%)
  waiting for transfers between devices  7.26 us (12%)
  between operations  0.78 us (1%)
  loops' own time  0.69 us (1%)
    ppermute x20, starting transfers between devices, run(): move = lambda x, pairs: lax.ppermute(x, names, pairs)  33.8 us
    pallas_call x9, Pallas kernels, call(): pl.pallas_call(kernel, out_shape=outs, in_specs=[smem] + [there if i in a...  17 us
    ppermute x20, waiting for transfers between devices, run(): move = lambda x, pairs: lax.ppermute(x, names, pairs)  7.26 us
  transfers between devices with their start and end apart: 20, of which 4 were waited for; matrix products, arithmetic and copies ran while one was open for 0% of the time, Pallas kernels for 12%

commit v1 on v0

--- a/solution.py
+++ b/solution.py
@@ -258,6 +258,10 @@
 def left_and_right(flags, a, b):
     even = flagged(flags, S_EVEN, a.shape)
     return jnp.where(even, b, a), jnp.where(even, a, b)
+
+
+def three(panels):
+    return [panels.at[:, :, pl.ds(LANES * i, LANES)] for i in range(3)]
 
 
 def widened(flags, own, a, b):
@@ -612,7 +616,8 @@
     settle(psi, outer, acc, keep, factor, pushed, base, False)
 
 
-def advance(flags, base, strip, from_a, from_b, zone_a, near, far, maps, factor, out):
+def advance(flags, base, strip, from_a, from_b, panels, maps, factor, out):
+    near, far, zone_a = three(panels)
     through = mapped_back(near[...], far[...], maps)
     even = flagged(flags, B_EVEN, (8, LANES))
     plane = flagged(flags, PLANE, (8, LANES))
@@ -633,15 +638,15 @@
 
 
 def step_kernel(
-    flags, base, strip, from_a, from_b, zone_a, near, far, maps, factor, cm, ch, cs, xf, ts,
+    flags, base, strip, from_a, from_b, panels, maps, factor, cm, ch, cs, xf, ts,
     psi, acc, strip_out, to_a, to_b, ghost,
 ):
-    advance(flags, base, strip, from_a, from_b, zone_a, near, far, maps, factor, psi)
+    advance(flags, base, strip, from_a, from_b, panels, maps, factor, psi)
     outer_terms(flags, psi, (cm, ch, cs, xf, ts), acc, strip_out, to_a, to_b, ghost)
 
 
-def last_kernel(flags, base, strip, from_a, from_b, zone_a, near, far, maps, factor, out):
-    advance(flags, base, strip, from_a, from_b, zone_a, near, far, maps, factor, out)
+def last_kernel(flags, base, strip, from_a, from_b, panels, maps, factor, out):
+    advance(flags, base, strip, from_a, from_b, panels, maps, factor, out)
 
 
 def f32(*shape):
@@ -732,7 +737,7 @@
                 move(to_b, near),
                 move(to_b, far),
             )
-            return moved if beside is None else moved + tuple(beside(*args))
+            return tuple(beside(moved, *args))
 
         return run
 
@@ -741,8 +746,8 @@
     )
 
 
-def first_beside(*args):
-    return call(
+def first_beside(moved, *args):
+    prepared = call(
         prepare_kernel,
         (f32(*MAPS), f32(*MAPS)) + FIXED + (f32(*STRIP), f32(*STATE)) + INNER + (SHARED,),
         args,
@@ -751,10 +756,13 @@
         away=(1,),
         copies=2,
     )
-
-
-def next_beside(*args):
-    return (call(inner_kernel, f32(*STATE), args, (STATE,), name="inner", in_place={2: 0}),)
+    return (*moved, *prepared)
+
+
+def next_beside(moved, *args):
+    a, b, block, near, far = moved
+    base = call(inner_kernel, f32(*STATE), args, (STATE,), name="inner", in_place={2: 0})
+    return a, b, jnp.concatenate([near, far, block], axis=2), base
 
 
 def shards(flow, adjoint, adjoint_later, objective_grad, volume, panel_maps, rotor_step, names):
@@ -814,7 +822,7 @@
         arrived = send(
             strip, to_a, to_b, beside=next_beside, args=(flags, psi, acc, keep, factor, pushed) + inner
         )
-        args = (flags, arrived[5], strip) + arrived[:5] + (maps, factor)
+        args = (flags, arrived[3], strip) + arrived[:3] + (maps, factor)
         if sweep == ITERS - 1:
             return call(last_kernel, f32(*STATE), args, name="last")
         terms = tuple(call(step_kernel, TERMS, args + (cm,) + outer, (GHOST,), name="step"))

time: 60.9 us -> 59.6 us (0.979)
  waiting for transfers between devices: 7.26 us -> 4.58 us
  starting transfers between devices: 33.8 us -> 35.7 us
    ppermute x20, waiting for transfers between devices: 7.26 us -> 4.58 us  [run(): move = lambda x, pairs: lax.ppermute(x, names, pairs)]
    ppermute x20, starting transfers between devices: 33.8 us -> 35.7 us  [run(): move = lambda x, pairs: lax.ppermute(x, names, pairs)]
where the time goes in v1:
time: 59.6 us; the launch traced here: 58.9 us
  starting transfers between devices  35.7 us (60%)
  Pallas kernels  16.8 us (28%)
  waiting for transfers between devices  4.58 us (8%)
  between operations  0.78 us (1%)
  loops' own time  0.74 us (1%)
    ppermute x20, starting transfers between devices, run(): move = lambda x, pairs: lax.ppermute(x, names, pairs)  35.7 us
    pallas_call x9, Pallas kernels, call(): pl.pallas_call(kernel, out_shape=outs, in_specs=[smem] + [there if i in a...  16.8 us
    ppermute x20, waiting for transfers between devices, run(): move = lambda x, pairs: lax.ppermute(x, names, pairs)  4.58 us
  transfers between devices with their start and end apart: 20, of which 4 were waited for; matrix products, arithmetic and copies ran while one was open for 0% of the time, Pallas kernels for 12%

profile of v1, /device:TPU:9, one launch (start us, length us, event | category | flops | bytes accessed | tf_op | source)
XLA Modules:
  0.0 58.9 jit_solution(13683321211520374530)
XLA Ops:
  0.9 1.1 %pack.1 = (f32[5,24,128]{2,1,0:T(8,128)S(1)}, f32[5,24,128]{2,1,0:T(8,128)S(1)}, f32[5,24,128]{2,1,0:T(8,128)S(1)}) custom-call(s32[8]{0:T(128)S(1)} %stack.55.flags, f32[5,4,16,128]{3,2,1,0:T(8,128)S(1)} %copy-done.1, f32[5,4,16,128]{3,2,1,0:T(8,128)} %adjoint.1), custom_call_target="tpu_custom_call" | custom-call | tf_op jit(solution)/shard_map/pack/pallas_call | solution.py:684
  2.1 14.4 %conditional.4 = (f32[5,24,128]{2,1,0:T(8,128)}, f32[5,24,128]{2,1,0:T(8,128)}, f32[5,24,128]{2,1,0:T(8,128)}, f32[5,24,128]{2,1,0:T(8,128)}, f32[5,24,128]{2,1,...) conditional(s32[]{:T(128)} %clamp.2, ...), branch_computations={%region_0.1_spmd, %region_1.2_spmd, %region_2.3_spmd, %region_3.4_... | conditional | bytes 1229136 | solution.py:745
  2.2 2.2 %collective-permute-start.21 = (f32[5,24,128]{2,1,0:T(8,128)S(1)}, f32[5,24,128]{2,1,0:T(8,128)}, u32[]{:S(2)}, u32[]{:S(2)}) collective-permute-start(f32[5,24,128]{2,1,0:T(8,128)S(1)} %get-tuple-element.877), channel_id=1, source_target_pairs={{0,28},{4,8},{8,4},{12,16},{16,12},{20,24},{24,20},{28,0},{1,29},{... | collective-permute-start | bytes 184328 | tf_op jit(solution)/shard_map/cond/branch_4_fun/ppermute | solution.py:732
  4.4 0.5 collective-permute-start.20
  4.9 5.1 %collective-permute-start.24 = (f32[5,24,128]{2,1,0:T(8,128)S(1)}, f32[5,24,128]{2,1,0:T(8,128)}, u32[]{:S(2)}, u32[]{:S(2)}) collective-permute-start(f32[5,24,128]{2,1,0:T(8,128)S(1)} %get-tuple-element.879), channel_id=1, source_target_pairs={{0,0},{4,4},{8,8},{12,12},{16,16},{20,20},{24,24},{28,28},{1,22},{... | collective-permute-start | bytes 184328 | tf_op jit(solution)/shard_map/cond/branch_4_fun/ppermute | solution.py:732
  10.0 1.9 %collective-permute-start.23 = (f32[5,24,128]{2,1,0:T(8,128)S(1)}, f32[5,24,128]{2,1,0:T(8,128)}, u32[]{:S(2)}, u32[]{:S(2)}) collective-permute-start(f32[5,24,128]{2,1,0:T(8,128)S(1)} %get-tuple-element.879), channel_id=1, source_target_pairs={{0,0},{4,4},{8,8},{12,12},{16,16},{20,20},{24,24},{28,28},{1,18},{... | collective-permute-start | bytes 184328 | tf_op jit(solution)/shard_map/cond/branch_4_fun/ppermute | solution.py:732
  11.9 3.8 %prepare.12 = (f32[2,128,128]{2,1,0:T(8,128)S(1)}, f32[2,128,128]{2,1,0:T(8,128)S(1)}, f32[4,16,128]{2,1,0:T(8,128)S(1)}, f32[4,16,128]{2,1,0:T(8,128)S(1)}, f32...) custom-call(s32[8]{0:T(128)S(1)} %get-tuple-element.880.flags, ...), custom_call_target="tpu_custom_call" | custom-call | tf_op jit(solution)/shard_map/cond/branch_4_fun/prepare/pallas_call | solution.py:684
  15.7 0.7 %collective-permute-done.23 = f32[5,24,128]{2,1,0:T(8,128)} collective-permute-done((f32[5,24,128]{2,1,0:T(8,128)S(1)}, f32[5,24,128]{2,1,0:T(8,128)}, u32[]{:S(2)}, u32[]{:S(2)}) %collective-permute-start.23) | collective-permute-done | bytes 61472 | tf_op jit(solution)/shard_map/cond/branch_4_fun/ppermute | solution.py:732
  16.4 3.4 %start.1 = (f32[5,4,16,128]{3,2,1,0:T(8,128)S(1)}, f32[5,4,16,128]{3,2,1,0:T(8,128)S(1)}, f32[5,16,128]{2,1,0:T(8,128)S(1)}, f32[5,8,128]{2,1,0:T(8,128)S(1)}, f...) custom-call(s32[8]{0:T(128)S(1)} %stack.55.flags, ...), custom_call_target="tpu_custom_call" | custom-call | tf_op jit(solution)/shard_map/start/pallas_call | solution.py:684
  19.9 11.1 %conditional.5 = (f32[5,16,128]{2,1,0:T(8,128)}, f32[5,16,128]{2,1,0:T(8,128)}, f32[5,8,384]{2,1,0:T(8,128)S(1)}, f32[5,4,16,128]{3,2,1,0:T(8,128)S(1)}) conditional(s32[]{:T(128)} %clamp.2, (f32[5,16,128]{2,1,0:T(8,128)S(1)}, f32[5,8,128]{2,1,0:T(8,128)S(1)}, f32[5,8,128]{2,1,0:T(8,128)S(1)}, s32[8]{0:T(128)S(1)}, ...), branch_computations={%region_8.9_spmd, %region_9.10_spmd, %region_10.11_spmd, %region_1... | conditional | flops 30720 | bytes 696552 | solution.py:745
  20.1 3.7 %collective-permute-start.63 = (f32[5,8,128]{2,1,0:T(8,128)S(1)}, f32[5,8,128]{2,1,0:T(8,128)S(1)}, u32[]{:S(2)}, u32[]{:S(2)}) collective-permute-start(f32[5,8,128]{2,1,0:T(8,128)S(1)} %get-tuple-element.1018), channel_id=1, source_target_pairs={{0,0},{4,4},{8,8},{12,12},{16,16},{20,20},{24,24},{28,28},{1,22},{... | collective-permute-start | bytes 61448 | tf_op jit(solution)/shard_map/cond/branch_4_fun/ppermute | solution.py:732
  23.9 3.2 %collective-permute-start.62 = (f32[5,8,128]{2,1,0:T(8,128)S(1)}, f32[5,8,128]{2,1,0:T(8,128)S(1)}, u32[]{:S(2)}, u32[]{:S(2)}) collective-permute-start(f32[5,8,128]{2,1,0:T(8,128)S(1)} %get-tuple-element.1018), channel_id=1, source_target_pairs={{0,0},{4,4},{8,8},{12,12},{16,16},{20,20},{24,24},{28,28},{1,18},{... | collective-permute-start | bytes 61448 | tf_op jit(solution)/shard_map/cond/branch_4_fun/ppermute | solution.py:732
  27.1 1.1 %collective-permute-start.61 = (f32[5,16,128]{2,1,0:T(8,128)S(1)}, f32[5,16,128]{2,1,0:T(8,128)}, u32[]{:S(2)}, u32[]{:S(2)}) collective-permute-start(f32[5,16,128]{2,1,0:T(8,128)S(1)} %get-tuple-element.1017), channel_id=1, source_target_pairs={{0,28},{4,8},{8,4},{12,16},{16,12},{20,24},{24,20},{28,0},{1,29},{... | collective-permute-start | bytes 122888 | tf_op jit(solution)/shard_map/cond/branch_4_fun/ppermute | solution.py:732
  28.1 0.7 %collective-permute-start.60 = (f32[5,16,128]{2,1,0:T(8,128)S(1)}, f32[5,16,128]{2,1,0:T(8,128)}, u32[]{:S(2)}, u32[]{:S(2)}) collective-permute-start(f32[5,16,128]{2,1,0:T(8,128)S(1)} %get-tuple-element.1017), channel_id=1, source_target_pairs={{0,4},{4,0},{8,12},{12,8},{16,20},{20,16},{24,28},{28,24},{1,5},{5... | collective-permute-start | bytes 122888 | tf_op jit(solution)/shard_map/cond/branch_4_fun/ppermute | solution.py:732
  28.8 1.1 %inner.28 = f32[5,4,16,128]{3,2,1,0:T(8,128)S(1)} custom-call(s32[8]{0:T(128)S(1)} %get-tuple-element.1020.flags, f32[5,4,16,128]{3,2,1,0:T(8,128)S(1)} %get-tuple-element.1021.psi, f32[5,4,16,128]{3,2,1,0:T(8,128)S(1)} %get-tuple-element.1022.outer, f32[4,16,128]{2,1,0:T(8,128)S(1)} %get-tuple-element.1023.keep, ...), custom_call_target="tpu_custom_call", output_to_operand_aliasing={{}: (2, {})} | custom-call | tf_op jit(solution)/shard_map/cond/branch_4_fun/inner/pallas_call | solution.py:684
  30.0 1.0 %collective-permute-done.61 = f32[5,16,128]{2,1,0:T(8,128)} collective-permute-done((f32[5,16,128]{2,1,0:T(8,128)S(1)}, f32[5,16,128]{2,1,0:T(8,128)}, u32[]{:S(2)}, u32[]{:S(2)}) %collective-permute-start.61) | collective-permute-done | bytes 40992 | tf_op jit(solution)/shard_map/cond/branch_4_fun/ppermute | solution.py:732
  31.0 1.7 %step.2 = (f32[5,4,16,128]{3,2,1,0:T(8,128)S(1)}, f32[5,4,16,128]{3,2,1,0:T(8,128)S(1)}, f32[5,16,128]{2,1,0:T(8,128)S(1)}, f32[5,8,128]{2,1,0:T(8,128)S(1)}, f32[5,8,128]{2,1,0:T(8,128)S(1)}) custom-call(s32[8]{0:T(128)S(1)} %stack.55.flags, f32[5,4,16,128]{3,2,1,0:T(8,128)S(1)} %get-tuple-element.1353.base, f32[5,16,128]{2,1,0:T(8,128)S(1)} %get-tuple-element.1343.strip, ...), custom_call_target="tpu_custom_call" | custom-call | tf_op jit(solution)/shard_map/step/pallas_call | solution.py:684
  32.7 10.9 %conditional.6 = (f32[5,16,128]{2,1,0:T(8,128)}, f32[5,16,128]{2,1,0:T(8,128)}, f32[5,8,384]{2,1,0:T(8,128)S(1)}, f32[5,4,16,128]{3,2,1,0:T(8,128)S(1)}) conditional(s32[]{:T(128)} %clamp.2, (f32[5,16,128]{2,1,0:T(8,128)S(1)}, f32[5,8,128]{2,1,0:T(8,128)S(1)}, f32[5,8,128]{2,1,0:T(8,128)S(1)}, s32[8]{0:T(128)S(1)}, ...), branch_computations={%region_16.17_spmd, %region_17.18_spmd, %region_18.19_spmd, %regio... | conditional | flops 30720 | bytes 696552 | solution.py:745
  32.8 3.3 %collective-permute-start.103 = (f32[5,8,128]{2,1,0:T(8,128)S(1)}, f32[5,8,128]{2,1,0:T(8,128)S(1)}, u32[]{:S(2)}, u32[]{:S(2)}) collective-permute-start(f32[5,8,128]{2,1,0:T(8,128)S(1)} %get-tuple-element.1122), channel_id=1, source_target_pairs={{0,0},{4,4},{8,8},{12,12},{16,16},{20,20},{24,24},{28,28},{1,22},{... | collective-permute-start | bytes 61448 | tf_op jit(solution)/shard_map/cond/branch_4_fun/ppermute | solution.py:732
  36.1 3.5 %collective-permute-start.102 = (f32[5,8,128]{2,1,0:T(8,128)S(1)}, f32[5,8,128]{2,1,0:T(8,128)S(1)}, u32[]{:S(2)}, u32[]{:S(2)}) collective-permute-start(f32[5,8,128]{2,1,0:T(8,128)S(1)} %get-tuple-element.1122), channel_id=1, source_target_pairs={{0,0},{4,4},{8,8},{12,12},{16,16},{20,20},{24,24},{28,28},{1,18},{... | collective-permute-start | bytes 61448 | tf_op jit(solution)/shard_map/cond/branch_4_fun/ppermute | solution.py:732
  39.6 1.2 %collective-permute-start.101 = (f32[5,16,128]{2,1,0:T(8,128)S(1)}, f32[5,16,128]{2,1,0:T(8,128)}, u32[]{:S(2)}, u32[]{:S(2)}) collective-permute-start(f32[5,16,128]{2,1,0:T(8,128)S(1)} %get-tuple-element.1121), channel_id=1, source_target_pairs={{0,28},{4,8},{8,4},{12,16},{16,12},{20,24},{24,20},{28,0},{1,29},{... | collective-permute-start | bytes 122888 | tf_op jit(solution)/shard_map/cond/branch_4_fun/ppermute | solution.py:732
  40.8 0.7 %collective-permute-start.100 = (f32[5,16,128]{2,1,0:T(8,128)S(1)}, f32[5,16,128]{2,1,0:T(8,128)}, u32[]{:S(2)}, u32[]{:S(2)}) collective-permute-start(f32[5,16,128]{2,1,0:T(8,128)S(1)} %get-tuple-element.1121), channel_id=1, source_target_pairs={{0,4},{4,0},{8,12},{12,8},{16,20},{20,16},{24,28},{28,24},{1,5},{5... | collective-permute-start | bytes 122888 | tf_op jit(solution)/shard_map/cond/branch_4_fun/ppermute | solution.py:732
  41.5 1.1 %inner.36 = f32[5,4,16,128]{3,2,1,0:T(8,128)S(1)} custom-call(s32[8]{0:T(128)S(1)} %get-tuple-element.1124.flags, f32[5,4,16,128]{3,2,1,0:T(8,128)S(1)} %get-tuple-element.1125.psi, f32[5,4,16,128]{3,2,1,0:T(8,128)S(1)} %get-tuple-element.1126.outer, f32[4,16,128]{2,1,0:T(8,128)S(1)} %get-tuple-element.1127.keep, ...), custom_call_target="tpu_custom_call", output_to_operand_aliasing={{}: (2, {})} | custom-call | tf_op jit(solution)/shard_map/cond/branch_4_fun/inner/pallas_call | solution.py:684
  42.7 0.9 %collective-permute-done.101 = f32[5,16,128]{2,1,0:T(8,128)} collective-permute-done((f32[5,16,128]{2,1,0:T(8,128)S(1)}, f32[5,16,128]{2,1,0:T(8,128)}, u32[]{:S(2)}, u32[]{:S(2)}) %collective-permute-start.101) | collective-permute-done | bytes 40992 | tf_op jit(solution)/shard_map/cond/branch_4_fun/ppermute | solution.py:732
  43.6 1.7 %step.3 = (f32[5,4,16,128]{3,2,1,0:T(8,128)S(1)}, f32[5,4,16,128]{3,2,1,0:T(8,128)S(1)}, f32[5,16,128]{2,1,0:T(8,128)S(1)}, f32[5,8,128]{2,1,0:T(8,128)S(1)}, f32[5,8,128]{2,1,0:T(8,128)S(1)}) custom-call(s32[8]{0:T(128)S(1)} %stack.55.flags, f32[5,4,16,128]{3,2,1,0:T(8,128)S(1)} %get-tuple-element.1366.base, f32[5,16,128]{2,1,0:T(8,128)S(1)} %get-tuple-element.1361.strip, ...), custom_call_target="tpu_custom_call" | custom-call | tf_op jit(solution)/shard_map/step/pallas_call | solution.py:684
  45.4 11.8 %conditional.7 = (f32[5,16,128]{2,1,0:T(8,128)}, f32[5,16,128]{2,1,0:T(8,128)}, f32[5,8,384]{2,1,0:T(8,128)S(1)}, f32[5,4,16,128]{3,2,1,0:T(8,128)S(1)}) conditional(s32[]{:T(128)} %clamp.2, (f32[5,16,128]{2,1,0:T(8,128)S(1)}, f32[5,8,128]{2,1,0:T(8,128)S(1)}, f32[5,8,128]{2,1,0:T(8,128)S(1)}, s32[8]{0:T(128)S(1)}, ...), branch_computations={%region_24.25_spmd, %region_25.26_spmd, %region_26.27_spmd, %regio... | conditional | flops 30720 | bytes 696552 | solution.py:745
  45.7 3.7 %collective-permute-start.143 = (f32[5,8,128]{2,1,0:T(8,128)S(1)}, f32[5,8,128]{2,1,0:T(8,128)S(1)}, u32[]{:S(2)}, u32[]{:S(2)}) collective-permute-start(f32[5,8,128]{2,1,0:T(8,128)S(1)} %get-tuple-element.1226), channel_id=1, source_target_pairs={{0,0},{4,4},{8,8},{12,12},{16,16},{20,20},{24,24},{28,28},{1,22},{... | collective-permute-start | bytes 61448 | tf_op jit(solution)/shard_map/cond/branch_4_fun/ppermute | solution.py:732
  49.4 3.6 %collective-permute-start.142 = (f32[5,8,128]{2,1,0:T(8,128)S(1)}, f32[5,8,128]{2,1,0:T(8,128)S(1)}, u32[]{:S(2)}, u32[]{:S(2)}) collective-permute-start(f32[5,8,128]{2,1,0:T(8,128)S(1)} %get-tuple-element.1226), channel_id=1, source_target_pairs={{0,0},{4,4},{8,8},{12,12},{16,16},{20,20},{24,24},{28,28},{1,18},{... | collective-permute-start | bytes 61448 | tf_op jit(solution)/shard_map/cond/branch_4_fun/ppermute | solution.py:732
  53.0 0.7 %collective-permute-start.141 = (f32[5,16,128]{2,1,0:T(8,128)S(1)}, f32[5,16,128]{2,1,0:T(8,128)}, u32[]{:S(2)}, u32[]{:S(2)}) collective-permute-start(f32[5,16,128]{2,1,0:T(8,128)S(1)} %get-tuple-element.1225), channel_id=1, source_target_pairs={{0,28},{4,8},{8,4},{12,16},{16,12},{20,24},{24,20},{28,0},{1,29},{... | collective-permute-start | bytes 122888 | tf_op jit(solution)/shard_map/cond/branch_4_fun/ppermute | solution.py:732
  54.1 1.1 %inner.44 = f32[5,4,16,128]{3,2,1,0:T(8,128)S(1)} custom-call(s32[8]{0:T(128)S(1)} %get-tuple-element.1228.flags, f32[5,4,16,128]{3,2,1,0:T(8,128)S(1)} %get-tuple-element.1229.psi, f32[5,4,16,128]{3,2,1,0:T(8,128)S(1)} %get-tuple-element.1230.outer, f32[4,16,128]{2,1,0:T(8,128)S(1)} %get-tuple-element.1231.keep, ...), custom_call_target="tpu_custom_call", output_to_operand_aliasing={{}: (2, {})} | custom-call | tf_op jit(solution)/shard_map/cond/branch_4_fun/inner/pallas_call | solution.py:684
  55.3 1.9 %collective-permute-done.141 = f32[5,16,128]{2,1,0:T(8,128)} collective-permute-done((f32[5,16,128]{2,1,0:T(8,128)S(1)}, f32[5,16,128]{2,1,0:T(8,128)}, u32[]{:S(2)}, u32[]{:S(2)}) %collective-permute-start.141) | collective-permute-done | bytes 40992 | tf_op jit(solution)/shard_map/cond/branch_4_fun/ppermute | solution.py:732
  57.1 1.7 %last.1 = f32[5,4,16,128]{3,2,1,0:T(8,128)} custom-call(s32[8]{0:T(128)S(1)} %stack.55.flags, f32[5,4,16,128]{3,2,1,0:T(8,128)S(1)} %get-tuple-element.1375.base, f32[5,16,128]{2,1,0:T(8,128)S(1)} %get-tuple-element.1370.strip, f32[5,16,128]{2,1,0:T(8,128)} %get-tuple-element.1376.from_a, f32[5,16,128]{2,1,0:T(8,128)} %get-tuple-element.1377.from_b, ...), custom_call_target="tpu_custom_call" | custom-call | tf_op jit(solution)/shard_map/last/pallas_call | solution.py:684
  (29 shorter events, 0.9 us)
Async XLA Ops:
  0.0 0.9 %copy-start.1 = (f32[5,4,16,128]{3,2,1,0:T(8,128)S(1)}, f32[5,4,16,128]{3,2,1,0:T(8,128)}, u32[]{:S(2)}) copy-start(f32[5,4,16,128]{3,2,1,0:T(8,128)} %flow.3) | copy-start | bytes 491524
  0.0 2.1 %copy-start = (f32[2,5,4,16,128]{4,3,2,1,0:T(8,128)S(1)}, f32[2,5,4,16,128]{4,3,2,1,0:T(8,128)}, u32[]{:S(2)}) copy-start(f32[2,5,4,16,128]{4,3,2,1,0:T(8,128)} %param.41) | copy-start | bytes 983044
  2.1 13.6 %collective-permute-start.22 = (f32[5,24,128]{2,1,0:T(8,128)S(1)}, f32[5,24,128]{2,1,0:T(8,128)}, u32[]{:S(2)}, u32[]{:S(2)}) collective-permute-start(f32[5,24,128]{2,1,0:T(8,128)S(1)} %get-tuple-element.878), channel_id=1, source_target_pairs={{0,1},{4,5},{8,9},{12,13},{16,17},{20,21},{24,25},{28,29},{1,0},{5... | collective-permute-start | bytes 184328 | tf_op jit(solution)/shard_map/cond/branch_4_fun/ppermute | solution.py:732
  2.2 13.5 %collective-permute-start.21 = (f32[5,24,128]{2,1,0:T(8,128)S(1)}, f32[5,24,128]{2,1,0:T(8,128)}, u32[]{:S(2)}, u32[]{:S(2)}) collective-permute-start(f32[5,24,128]{2,1,0:T(8,128)S(1)} %get-tuple-element.877), channel_id=1, source_target_pairs={{0,28},{4,8},{8,4},{12,16},{16,12},{20,24},{24,20},{28,0},{1,29},{... | collective-permute-start | bytes 184328 | tf_op jit(solution)/shard_map/cond/branch_4_fun/ppermute | solution.py:732
  4.4 11.3 %collective-permute-start.20 = (f32[5,24,128]{2,1,0:T(8,128)S(1)}, f32[5,24,128]{2,1,0:T(8,128)}, u32[]{:S(2)}, u32[]{:S(2)}) collective-permute-start(f32[5,24,128]{2,1,0:T(8,128)S(1)} %get-tuple-element.877), channel_id=1, source_target_pairs={{0,4},{4,0},{8,12},{12,8},{16,20},{20,16},{24,28},{28,24},{1,5},{5... | collective-permute-start | bytes 184328 | tf_op jit(solution)/shard_map/cond/branch_4_fun/ppermute | solution.py:732
  4.9 10.8 %collective-permute-start.24 = (f32[5,24,128]{2,1,0:T(8,128)S(1)}, f32[5,24,128]{2,1,0:T(8,128)}, u32[]{:S(2)}, u32[]{:S(2)}) collective-permute-start(f32[5,24,128]{2,1,0:T(8,128)S(1)} %get-tuple-element.879), channel_id=1, source_target_pairs={{0,0},{4,4},{8,8},{12,12},{16,16},{20,20},{24,24},{28,28},{1,22},{... | collective-permute-start | bytes 184328 | tf_op jit(solution)/shard_map/cond/branch_4_fun/ppermute | solution.py:732
  10.0 6.5 %collective-permute-start.23 = (f32[5,24,128]{2,1,0:T(8,128)S(1)}, f32[5,24,128]{2,1,0:T(8,128)}, u32[]{:S(2)}, u32[]{:S(2)}) collective-permute-start(f32[5,24,128]{2,1,0:T(8,128)S(1)} %get-tuple-element.879), channel_id=1, source_target_pairs={{0,0},{4,4},{8,8},{12,12},{16,16},{20,20},{24,24},{28,28},{1,18},{... | collective-permute-start | bytes 184328 | tf_op jit(solution)/shard_map/cond/branch_4_fun/ppermute | solution.py:732
  20.1 9.9 %collective-permute-start.64 = (f32[5,8,128]{2,1,0:T(8,128)S(1)}, f32[5,8,128]{2,1,0:T(8,128)S(1)}, u32[]{:S(2)}, u32[]{:S(2)}) collective-permute-start(f32[5,8,128]{2,1,0:T(8,128)S(1)} %get-tuple-element.1019), channel_id=1, source_target_pairs={{0,1},{4,5},{8,9},{12,13},{16,17},{20,21},{24,25},{28,29},{1,0},{5... | collective-permute-start | bytes 61448 | tf_op jit(solution)/shard_map/cond/branch_4_fun/ppermute | solution.py:732
  20.1 9.8 %collective-permute-start.63 = (f32[5,8,128]{2,1,0:T(8,128)S(1)}, f32[5,8,128]{2,1,0:T(8,128)S(1)}, u32[]{:S(2)}, u32[]{:S(2)}) collective-permute-start(f32[5,8,128]{2,1,0:T(8,128)S(1)} %get-tuple-element.1018), channel_id=1, source_target_pairs={{0,0},{4,4},{8,8},{12,12},{16,16},{20,20},{24,24},{28,28},{1,22},{... | collective-permute-start | bytes 61448 | tf_op jit(solution)/shard_map/cond/branch_4_fun/ppermute | solution.py:732
  23.9 6.1 %collective-permute-start.62 = (f32[5,8,128]{2,1,0:T(8,128)S(1)}, f32[5,8,128]{2,1,0:T(8,128)S(1)}, u32[]{:S(2)}, u32[]{:S(2)}) collective-permute-start(f32[5,8,128]{2,1,0:T(8,128)S(1)} %get-tuple-element.1018), channel_id=1, source_target_pairs={{0,0},{4,4},{8,8},{12,12},{16,16},{20,20},{24,24},{28,28},{1,18},{... | collective-permute-start | bytes 61448 | tf_op jit(solution)/shard_map/cond/branch_4_fun/ppermute | solution.py:732
  27.1 3.9 %collective-permute-start.61 = (f32[5,16,128]{2,1,0:T(8,128)S(1)}, f32[5,16,128]{2,1,0:T(8,128)}, u32[]{:S(2)}, u32[]{:S(2)}) collective-permute-start(f32[5,16,128]{2,1,0:T(8,128)S(1)} %get-tuple-element.1017), channel_id=1, source_target_pairs={{0,28},{4,8},{8,4},{12,16},{16,12},{20,24},{24,20},{28,0},{1,29},{... | collective-permute-start | bytes 122888 | tf_op jit(solution)/shard_map/cond/branch_4_fun/ppermute | solution.py:732
  28.1 2.8 %collective-permute-start.60 = (f32[5,16,128]{2,1,0:T(8,128)S(1)}, f32[5,16,128]{2,1,0:T(8,128)}, u32[]{:S(2)}, u32[]{:S(2)}) collective-permute-start(f32[5,16,128]{2,1,0:T(8,128)S(1)} %get-tuple-element.1017), channel_id=1, source_target_pairs={{0,4},{4,0},{8,12},{12,8},{16,20},{20,16},{24,28},{28,24},{1,5},{5... | collective-permute-start | bytes 122888 | tf_op jit(solution)/shard_map/cond/branch_4_fun/ppermute | solution.py:732
  32.7 9.9 %collective-permute-start.104 = (f32[5,8,128]{2,1,0:T(8,128)S(1)}, f32[5,8,128]{2,1,0:T(8,128)S(1)}, u32[]{:S(2)}, u32[]{:S(2)}) collective-permute-start(f32[5,8,128]{2,1,0:T(8,128)S(1)} %get-tuple-element.1123), channel_id=1, source_target_pairs={{0,1},{4,5},{8,9},{12,13},{16,17},{20,21},{24,25},{28,29},{1,0},{5... | collective-permute-start | bytes 61448 | tf_op jit(solution)/shard_map/cond/branch_4_fun/ppermute | solution.py:732
  32.8 9.9 %collective-permute-start.103 = (f32[5,8,128]{2,1,0:T(8,128)S(1)}, f32[5,8,128]{2,1,0:T(8,128)S(1)}, u32[]{:S(2)}, u32[]{:S(2)}) collective-permute-start(f32[5,8,128]{2,1,0:T(8,128)S(1)} %get-tuple-element.1122), channel_id=1, source_target_pairs={{0,0},{4,4},{8,8},{12,12},{16,16},{20,20},{24,24},{28,28},{1,22},{... | collective-permute-start | bytes 61448 | tf_op jit(solution)/shard_map/cond/branch_4_fun/ppermute | solution.py:732
  36.1 6.6 %collective-permute-start.102 = (f32[5,8,128]{2,1,0:T(8,128)S(1)}, f32[5,8,128]{2,1,0:T(8,128)S(1)}, u32[]{:S(2)}, u32[]{:S(2)}) collective-permute-start(f32[5,8,128]{2,1,0:T(8,128)S(1)} %get-tuple-element.1122), channel_id=1, source_target_pairs={{0,0},{4,4},{8,8},{12,12},{16,16},{20,20},{24,24},{28,28},{1,18},{... | collective-permute-start | bytes 61448 | tf_op jit(solution)/shard_map/cond/branch_4_fun/ppermute | solution.py:732
  39.6 4.0 %collective-permute-start.101 = (f32[5,16,128]{2,1,0:T(8,128)S(1)}, f32[5,16,128]{2,1,0:T(8,128)}, u32[]{:S(2)}, u32[]{:S(2)}) collective-permute-start(f32[5,16,128]{2,1,0:T(8,128)S(1)} %get-tuple-element.1121), channel_id=1, source_target_pairs={{0,28},{4,8},{8,4},{12,16},{16,12},{20,24},{24,20},{28,0},{1,29},{... | collective-permute-start | bytes 122888 | tf_op jit(solution)/shard_map/cond/branch_4_fun/ppermute | solution.py:732
  40.8 2.8 %collective-permute-start.100 = (f32[5,16,128]{2,1,0:T(8,128)S(1)}, f32[5,16,128]{2,1,0:T(8,128)}, u32[]{:S(2)}, u32[]{:S(2)}) collective-permute-start(f32[5,16,128]{2,1,0:T(8,128)S(1)} %get-tuple-element.1121), channel_id=1, source_target_pairs={{0,4},{4,0},{8,12},{12,8},{16,20},{20,16},{24,28},{28,24},{1,5},{5... | collective-permute-start | bytes 122888 | tf_op jit(solution)/shard_map/cond/branch_4_fun/ppermute | solution.py:732
  45.6 9.6 %collective-permute-start.144 = (f32[5,8,128]{2,1,0:T(8,128)S(1)}, f32[5,8,128]{2,1,0:T(8,128)S(1)}, u32[]{:S(2)}, u32[]{:S(2)}) collective-permute-start(f32[5,8,128]{2,1,0:T(8,128)S(1)} %get-tuple-element.1227), channel_id=1, source_target_pairs={{0,1},{4,5},{8,9},{12,13},{16,17},{20,21},{24,25},{28,29},{1,0},{5... | collective-permute-start | bytes 61448 | tf_op jit(solution)/shard_map/cond/branch_4_fun/ppermute | solution.py:732
  45.7 9.5 %collective-permute-start.143 = (f32[5,8,128]{2,1,0:T(8,128)S(1)}, f32[5,8,128]{2,1,0:T(8,128)S(1)}, u32[]{:S(2)}, u32[]{:S(2)}) collective-permute-start(f32[5,8,128]{2,1,0:T(8,128)S(1)} %get-tuple-element.1226), channel_id=1, source_target_pairs={{0,0},{4,4},{8,8},{12,12},{16,16},{20,20},{24,24},{28,28},{1,22},{... | collective-permute-start | bytes 61448 | tf_op jit(solution)/shard_map/cond/branch_4_fun/ppermute | solution.py:732
  49.4 5.9 %collective-permute-start.142 = (f32[5,8,128]{2,1,0:T(8,128)S(1)}, f32[5,8,128]{2,1,0:T(8,128)S(1)}, u32[]{:S(2)}, u32[]{:S(2)}) collective-permute-start(f32[5,8,128]{2,1,0:T(8,128)S(1)} %get-tuple-element.1226), channel_id=1, source_target_pairs={{0,0},{4,4},{8,8},{12,12},{16,16},{20,20},{24,24},{28,28},{1,18},{... | collective-permute-start | bytes 61448 | tf_op jit(solution)/shard_map/cond/branch_4_fun/ppermute | solution.py:732
  53.0 4.2 %collective-permute-start.141 = (f32[5,16,128]{2,1,0:T(8,128)S(1)}, f32[5,16,128]{2,1,0:T(8,128)}, u32[]{:S(2)}, u32[]{:S(2)}) collective-permute-start(f32[5,16,128]{2,1,0:T(8,128)S(1)} %get-tuple-element.1225), channel_id=1, source_target_pairs={{0,28},{4,8},{8,4},{12,16},{16,12},{20,24},{24,20},{28,0},{1,29},{... | collective-permute-start | bytes 122888 | tf_op jit(solution)/shard_map/cond/branch_4_fun/ppermute | solution.py:732
  53.7 3.5 %collective-permute-start.140 = (f32[5,16,128]{2,1,0:T(8,128)S(1)}, f32[5,16,128]{2,1,0:T(8,128)}, u32[]{:S(2)}, u32[]{:S(2)}) collective-permute-start(f32[5,16,128]{2,1,0:T(8,128)S(1)} %get-tuple-element.1225), channel_id=1, source_target_pairs={{0,4},{4,0},{8,12},{12,8},{16,20},{20,16},{24,28},{28,24},{1,5},{5... | collective-permute-start | bytes 122888 | tf_op jit(solution)/shard_map/cond/branch_4_fun/ppermute | solution.py:732

commit v2 on v1

--- a/solution.py
+++ b/solution.py
@@ -617,7 +617,7 @@
 
 
 def advance(flags, base, strip, from_a, from_b, panels, maps, factor, out):
-    near, far, zone_a = three(panels)
+    zone_a, far, near = three(panels)
     through = mapped_back(near[...], far[...], maps)
     even = flagged(flags, B_EVEN, (8, LANES))
     plane = flagged(flags, PLANE, (8, LANES))
@@ -762,7 +762,7 @@
 def next_beside(moved, *args):
     a, b, block, near, far = moved
     base = call(inner_kernel, f32(*STATE), args, (STATE,), name="inner", in_place={2: 0})
-    return a, b, jnp.concatenate([near, far, block], axis=2), base
+    return a, b, jnp.concatenate([block, far, near], axis=2), base
 
 
 def shards(flow, adjoint, adjoint_later, objective_grad, volume, panel_maps, rotor_step, names):

time: 59.6 us -> 59.4 us (level)
  starting transfers between devices: 35.7 us -> 37.2 us
  waiting for transfers between devices: 4.58 us -> 3.25 us
    ppermute x20, starting transfers between devices: 35.7 us -> 37.2 us  [run(): move = lambda x, pairs: lax.ppermute(x, names, pairs)]
    ppermute x20, waiting for transfers between devices: 4.58 us -> 3.25 us  [run(): move = lambda x, pairs: lax.ppermute(x, names, pairs)]
  transfers between devices with their start and end apart: 20 -> 20, of which waited for: 4 -> 5; matrix products, arithmetic and copies ran while one was open for 0% -> 0% of each run, Pallas kernels for 12% -> 12%
where the time goes in v2:
time: 59.4 us; the launch traced here: 59.1 us
  starting transfers between devices  37.2 us (63%)
  Pallas kernels  16.8 us (28%)
  waiting for transfers between devices  3.25 us (5%)
  between operations  0.78 us (1%)
  loops' own time  0.76 us (1%)
    ppermute x20, starting transfers between devices, run(): move = lambda x, pairs: lax.ppermute(x, names, pairs)  37.2 us
    pallas_call x9, Pallas kernels, call(): pl.pallas_call(kernel, out_shape=outs, in_specs=[smem] + [there if i in a...  16.8 us
    ppermute x20, waiting for transfers between devices, run(): move = lambda x, pairs: lax.ppermute(x, names, pairs)  3.25 us
  transfers between devices with their start and end apart: 20, of which 5 were waited for; matrix products, arithmetic and copies ran while one was open for 0% of the time, Pallas kernels for 12%

profile of v2, /device:TPU:9, one launch (start us, length us, event | category | flops | bytes accessed | tf_op | source)
XLA Modules:
  0.0 59.1 jit_solution(11706424414697143209)
XLA Ops:
  0.9 1.1 %pack.1 = (f32[5,24,128]{2,1,0:T(8,128)S(1)}, f32[5,24,128]{2,1,0:T(8,128)S(1)}, f32[5,24,128]{2,1,0:T(8,128)S(1)}) custom-call(s32[8]{0:T(128)S(1)} %stack.55.flags, f32[5,4,16,128]{3,2,1,0:T(8,128)S(1)} %copy-done.1, f32[5,4,16,128]{3,2,1,0:T(8,128)} %adjoint.1), custom_call_target="tpu_custom_call" | custom-call | tf_op jit(solution)/shard_map/pack/pallas_call | solution.py:684
  2.1 15.2 %conditional.4 = (f32[5,24,128]{2,1,0:T(8,128)}, f32[5,24,128]{2,1,0:T(8,128)}, f32[5,24,128]{2,1,0:T(8,128)}, f32[5,24,128]{2,1,0:T(8,128)}, f32[5,24,128]{2,1,...) conditional(s32[]{:T(128)} %clamp.2, ...), branch_computations={%region_0.1_spmd, %region_1.2_spmd, %region_2.3_spmd, %region_3.4_... | conditional | bytes 1229136 | solution.py:745
  2.2 2.2 %collective-permute-start.26 = (f32[5,24,128]{2,1,0:T(8,128)S(1)}, f32[5,24,128]{2,1,0:T(8,128)}, u32[]{:S(2)}, u32[]{:S(2)}) collective-permute-start(f32[5,24,128]{2,1,0:T(8,128)S(1)} %get-tuple-element.899), channel_id=1, source_target_pairs={{0,28},{4,8},{8,4},{12,16},{16,12},{20,24},{24,20},{28,0},{1,29},{... | collective-permute-start | bytes 184328 | tf_op jit(solution)/shard_map/cond/branch_5_fun/ppermute | solution.py:732
  4.4 0.5 collective-permute-start.25
  4.9 4.7 %collective-permute-start.29 = (f32[5,24,128]{2,1,0:T(8,128)S(1)}, f32[5,24,128]{2,1,0:T(8,128)}, u32[]{:S(2)}, u32[]{:S(2)}) collective-permute-start(f32[5,24,128]{2,1,0:T(8,128)S(1)} %get-tuple-element.901), channel_id=1, source_target_pairs={{0,0},{4,4},{8,8},{12,12},{16,16},{20,20},{24,24},{28,28},{1,26},{... | collective-permute-start | bytes 184328 | tf_op jit(solution)/shard_map/cond/branch_5_fun/ppermute | solution.py:732
  9.6 2.6 %collective-permute-start.28 = (f32[5,24,128]{2,1,0:T(8,128)S(1)}, f32[5,24,128]{2,1,0:T(8,128)}, u32[]{:S(2)}, u32[]{:S(2)}) collective-permute-start(f32[5,24,128]{2,1,0:T(8,128)S(1)} %get-tuple-element.901), channel_id=1, source_target_pairs={{0,0},{4,4},{8,8},{12,12},{16,16},{20,20},{24,24},{28,28},{1,22},{... | collective-permute-start | bytes 184328 | tf_op jit(solution)/shard_map/cond/branch_5_fun/ppermute | solution.py:732
  12.2 3.8 %prepare.13 = (f32[2,128,128]{2,1,0:T(8,128)S(1)}, f32[2,128,128]{2,1,0:T(8,128)S(1)}, f32[4,16,128]{2,1,0:T(8,128)S(1)}, f32[4,16,128]{2,1,0:T(8,128)S(1)}, f32...) custom-call(s32[8]{0:T(128)S(1)} %get-tuple-element.902.flags, ...), custom_call_target="tpu_custom_call" | custom-call | tf_op jit(solution)/shard_map/cond/branch_5_fun/prepare/pallas_call | solution.py:684
  16.0 1.3 %collective-permute-done.28 = f32[5,24,128]{2,1,0:T(8,128)} collective-permute-done((f32[5,24,128]{2,1,0:T(8,128)S(1)}, f32[5,24,128]{2,1,0:T(8,128)}, u32[]{:S(2)}, u32[]{:S(2)}) %collective-permute-start.28) | collective-permute-done | bytes 61472 | tf_op jit(solution)/shard_map/cond/branch_5_fun/ppermute | solution.py:732
  17.3 3.4 %start.1 = (f32[5,4,16,128]{3,2,1,0:T(8,128)S(1)}, f32[5,4,16,128]{3,2,1,0:T(8,128)S(1)}, f32[5,16,128]{2,1,0:T(8,128)S(1)}, f32[5,8,128]{2,1,0:T(8,128)S(1)}, f...) custom-call(s32[8]{0:T(128)S(1)} %stack.55.flags, ...), custom_call_target="tpu_custom_call" | custom-call | tf_op jit(solution)/shard_map/start/pallas_call | solution.py:684
  20.7 10.2 %conditional.5 = (f32[5,16,128]{2,1,0:T(8,128)}, f32[5,16,128]{2,1,0:T(8,128)}, f32[5,8,384]{2,1,0:T(8,128)S(1)}, f32[5,4,16,128]{3,2,1,0:T(8,128)S(1)}) conditional(s32[]{:T(128)} %clamp.2, (f32[5,16,128]{2,1,0:T(8,128)S(1)}, f32[5,8,128]{2,1,0:T(8,128)S(1)}, f32[5,8,128]{2,1,0:T(8,128)S(1)}, s32[8]{0:T(128)S(1)}, ...), branch_computations={%region_8.9_spmd, %region_9.10_spmd, %region_10.11_spmd, %region_1... | conditional | flops 30720 | bytes 696552 | solution.py:745
  21.0 3.5 %collective-permute-start.69 = (f32[5,8,128]{2,1,0:T(8,128)S(1)}, f32[5,8,128]{2,1,0:T(8,128)S(1)}, u32[]{:S(2)}, u32[]{:S(2)}) collective-permute-start(f32[5,8,128]{2,1,0:T(8,128)S(1)} %get-tuple-element.1032), channel_id=1, source_target_pairs={{0,0},{4,4},{8,8},{12,12},{16,16},{20,20},{24,24},{28,28},{1,22},{... | collective-permute-start | bytes 61448 | tf_op jit(solution)/shard_map/cond/branch_5_fun/ppermute | solution.py:732
  24.5 2.2 %collective-permute-start.68 = (f32[5,8,128]{2,1,0:T(8,128)S(1)}, f32[5,8,128]{2,1,0:T(8,128)S(1)}, u32[]{:S(2)}, u32[]{:S(2)}) collective-permute-start(f32[5,8,128]{2,1,0:T(8,128)S(1)} %get-tuple-element.1032), channel_id=1, source_target_pairs={{0,0},{4,4},{8,8},{12,12},{16,16},{20,20},{24,24},{28,28},{1,26},{... | collective-permute-start | bytes 61448 | tf_op jit(solution)/shard_map/cond/branch_5_fun/ppermute | solution.py:732
  26.7 0.9 %collective-permute-start.66 = (f32[5,16,128]{2,1,0:T(8,128)S(1)}, f32[5,16,128]{2,1,0:T(8,128)}, u32[]{:S(2)}, u32[]{:S(2)}) collective-permute-start(f32[5,16,128]{2,1,0:T(8,128)S(1)} %get-tuple-element.1030), channel_id=1, source_target_pairs={{0,28},{4,8},{8,4},{12,16},{16,12},{20,24},{24,20},{28,0},{1,29},{... | collective-permute-start | bytes 122888 | tf_op jit(solution)/shard_map/cond/branch_5_fun/ppermute | solution.py:732
  27.7 1.6 %collective-permute-start.65 = (f32[5,16,128]{2,1,0:T(8,128)S(1)}, f32[5,16,128]{2,1,0:T(8,128)}, u32[]{:S(2)}, u32[]{:S(2)}) collective-permute-start(f32[5,16,128]{2,1,0:T(8,128)S(1)} %get-tuple-element.1030), channel_id=1, source_target_pairs={{0,4},{4,0},{8,12},{12,8},{16,20},{20,16},{24,28},{28,24},{1,5},{5... | collective-permute-start | bytes 122888 | tf_op jit(solution)/shard_map/cond/branch_5_fun/ppermute | solution.py:732
  29.3 1.1 %inner.29 = f32[5,4,16,128]{3,2,1,0:T(8,128)S(1)} custom-call(s32[8]{0:T(128)S(1)} %get-tuple-element.1033.flags, f32[5,4,16,128]{3,2,1,0:T(8,128)S(1)} %get-tuple-element.1034.psi, f32[5,4,16,128]{3,2,1,0:T(8,128)S(1)} %get-tuple-element.1035.outer, f32[4,16,128]{2,1,0:T(8,128)S(1)} %get-tuple-element.1036.keep, ...), custom_call_target="tpu_custom_call", output_to_operand_aliasing={{}: (2, {})} | custom-call | tf_op jit(solution)/shard_map/cond/branch_5_fun/inner/pallas_call | solution.py:684
  30.4 0.5 collective-permute-done.68
  30.9 1.7 %step.2 = (f32[5,4,16,128]{3,2,1,0:T(8,128)S(1)}, f32[5,4,16,128]{3,2,1,0:T(8,128)S(1)}, f32[5,16,128]{2,1,0:T(8,128)S(1)}, f32[5,8,128]{2,1,0:T(8,128)S(1)}, f32[5,8,128]{2,1,0:T(8,128)S(1)}) custom-call(s32[8]{0:T(128)S(1)} %stack.55.flags, f32[5,4,16,128]{3,2,1,0:T(8,128)S(1)} %get-tuple-element.1353.base, f32[5,16,128]{2,1,0:T(8,128)S(1)} %get-tuple-element.1343.strip, ...), custom_call_target="tpu_custom_call" | custom-call | tf_op jit(solution)/shard_map/step/pallas_call | solution.py:684
  32.6 12.2 %conditional.6 = (f32[5,16,128]{2,1,0:T(8,128)}, f32[5,16,128]{2,1,0:T(8,128)}, f32[5,8,384]{2,1,0:T(8,128)S(1)}, f32[5,4,16,128]{3,2,1,0:T(8,128)S(1)}) conditional(s32[]{:T(128)} %clamp.2, (f32[5,16,128]{2,1,0:T(8,128)S(1)}, f32[5,8,128]{2,1,0:T(8,128)S(1)}, f32[5,8,128]{2,1,0:T(8,128)S(1)}, s32[8]{0:T(128)S(1)}, ...), branch_computations={%region_16.17_spmd, %region_17.18_spmd, %region_18.19_spmd, %regio... | conditional | flops 30720 | bytes 696552 | solution.py:745
  32.7 5.0 %collective-permute-start.109 = (f32[5,8,128]{2,1,0:T(8,128)S(1)}, f32[5,8,128]{2,1,0:T(8,128)S(1)}, u32[]{:S(2)}, u32[]{:S(2)}) collective-permute-start(f32[5,8,128]{2,1,0:T(8,128)S(1)} %get-tuple-element.1136), channel_id=1, source_target_pairs={{0,0},{4,4},{8,8},{12,12},{16,16},{20,20},{24,24},{28,28},{1,22},{... | collective-permute-start | bytes 61448 | tf_op jit(solution)/shard_map/cond/branch_5_fun/ppermute | solution.py:732
  37.7 2.5 %collective-permute-start.108 = (f32[5,8,128]{2,1,0:T(8,128)S(1)}, f32[5,8,128]{2,1,0:T(8,128)S(1)}, u32[]{:S(2)}, u32[]{:S(2)}) collective-permute-start(f32[5,8,128]{2,1,0:T(8,128)S(1)} %get-tuple-element.1136), channel_id=1, source_target_pairs={{0,0},{4,4},{8,8},{12,12},{16,16},{20,20},{24,24},{28,28},{1,26},{... | collective-permute-start | bytes 61448 | tf_op jit(solution)/shard_map/cond/branch_5_fun/ppermute | solution.py:732
  40.2 1.1 %collective-permute-start.106 = (f32[5,16,128]{2,1,0:T(8,128)S(1)}, f32[5,16,128]{2,1,0:T(8,128)}, u32[]{:S(2)}, u32[]{:S(2)}) collective-permute-start(f32[5,16,128]{2,1,0:T(8,128)S(1)} %get-tuple-element.1134), channel_id=1, source_target_pairs={{0,28},{4,8},{8,4},{12,16},{16,12},{20,24},{24,20},{28,0},{1,29},{... | collective-permute-start | bytes 122888 | tf_op jit(solution)/shard_map/cond/branch_5_fun/ppermute | solution.py:732
  41.3 1.5 %collective-permute-start.105 = (f32[5,16,128]{2,1,0:T(8,128)S(1)}, f32[5,16,128]{2,1,0:T(8,128)}, u32[]{:S(2)}, u32[]{:S(2)}) collective-permute-start(f32[5,16,128]{2,1,0:T(8,128)S(1)} %get-tuple-element.1134), channel_id=1, source_target_pairs={{0,4},{4,0},{8,12},{12,8},{16,20},{20,16},{24,28},{28,24},{1,5},{5... | collective-permute-start | bytes 122888 | tf_op jit(solution)/shard_map/cond/branch_5_fun/ppermute | solution.py:732
  42.8 1.1 %inner.37 = f32[5,4,16,128]{3,2,1,0:T(8,128)S(1)} custom-call(s32[8]{0:T(128)S(1)} %get-tuple-element.1137.flags, f32[5,4,16,128]{3,2,1,0:T(8,128)S(1)} %get-tuple-element.1138.psi, f32[5,4,16,128]{3,2,1,0:T(8,128)S(1)} %get-tuple-element.1139.outer, f32[4,16,128]{2,1,0:T(8,128)S(1)} %get-tuple-element.1140.keep, ...), custom_call_target="tpu_custom_call", output_to_operand_aliasing={{}: (2, {})} | custom-call | tf_op jit(solution)/shard_map/cond/branch_5_fun/inner/pallas_call | solution.py:684
  44.1 0.7 %collective-permute-done.106 = f32[5,16,128]{2,1,0:T(8,128)} collective-permute-done((f32[5,16,128]{2,1,0:T(8,128)S(1)}, f32[5,16,128]{2,1,0:T(8,128)}, u32[]{:S(2)}, u32[]{:S(2)}) %collective-permute-start.106) | collective-permute-done | bytes 40992 | tf_op jit(solution)/shard_map/cond/branch_5_fun/ppermute | solution.py:732
  44.8 1.7 %step.3 = (f32[5,4,16,128]{3,2,1,0:T(8,128)S(1)}, f32[5,4,16,128]{3,2,1,0:T(8,128)S(1)}, f32[5,16,128]{2,1,0:T(8,128)S(1)}, f32[5,8,128]{2,1,0:T(8,128)S(1)}, f32[5,8,128]{2,1,0:T(8,128)S(1)}) custom-call(s32[8]{0:T(128)S(1)} %stack.55.flags, f32[5,4,16,128]{3,2,1,0:T(8,128)S(1)} %get-tuple-element.1366.base, f32[5,16,128]{2,1,0:T(8,128)S(1)} %get-tuple-element.1361.strip, ...), custom_call_target="tpu_custom_call" | custom-call | tf_op jit(solution)/shard_map/step/pallas_call | solution.py:684
  46.5 10.8 %conditional.7 = (f32[5,16,128]{2,1,0:T(8,128)}, f32[5,16,128]{2,1,0:T(8,128)}, f32[5,8,384]{2,1,0:T(8,128)S(1)}, f32[5,4,16,128]{3,2,1,0:T(8,128)S(1)}) conditional(s32[]{:T(128)} %clamp.2, (f32[5,16,128]{2,1,0:T(8,128)S(1)}, f32[5,8,128]{2,1,0:T(8,128)S(1)}, f32[5,8,128]{2,1,0:T(8,128)S(1)}, s32[8]{0:T(128)S(1)}, ...), branch_computations={%region_24.25_spmd, %region_25.26_spmd, %region_26.27_spmd, %regio... | conditional | flops 30720 | bytes 696552 | solution.py:745
  46.9 3.3 %collective-permute-start.149 = (f32[5,8,128]{2,1,0:T(8,128)S(1)}, f32[5,8,128]{2,1,0:T(8,128)S(1)}, u32[]{:S(2)}, u32[]{:S(2)}) collective-permute-start(f32[5,8,128]{2,1,0:T(8,128)S(1)} %get-tuple-element.1240), channel_id=1, source_target_pairs={{0,0},{4,4},{8,8},{12,12},{16,16},{20,20},{24,24},{28,28},{1,22},{... | collective-permute-start | bytes 61448 | tf_op jit(solution)/shard_map/cond/branch_5_fun/ppermute | solution.py:732
  50.2 3.1 %collective-permute-start.148 = (f32[5,8,128]{2,1,0:T(8,128)S(1)}, f32[5,8,128]{2,1,0:T(8,128)S(1)}, u32[]{:S(2)}, u32[]{:S(2)}) collective-permute-start(f32[5,8,128]{2,1,0:T(8,128)S(1)} %get-tuple-element.1240), channel_id=1, source_target_pairs={{0,0},{4,4},{8,8},{12,12},{16,16},{20,20},{24,24},{28,28},{1,26},{... | collective-permute-start | bytes 61448 | tf_op jit(solution)/shard_map/cond/branch_5_fun/ppermute | solution.py:732
  53.3 2.2 %collective-permute-start.146 = (f32[5,16,128]{2,1,0:T(8,128)S(1)}, f32[5,16,128]{2,1,0:T(8,128)}, u32[]{:S(2)}, u32[]{:S(2)}) collective-permute-start(f32[5,16,128]{2,1,0:T(8,128)S(1)} %get-tuple-element.1238), channel_id=1, source_target_pairs={{0,28},{4,8},{8,4},{12,16},{16,12},{20,24},{24,20},{28,0},{1,29},{... | collective-permute-start | bytes 122888 | tf_op jit(solution)/shard_map/cond/branch_5_fun/ppermute | solution.py:732
  55.6 1.1 %inner.45 = f32[5,4,16,128]{3,2,1,0:T(8,128)S(1)} custom-call(s32[8]{0:T(128)S(1)} %get-tuple-element.1241.flags, f32[5,4,16,128]{3,2,1,0:T(8,128)S(1)} %get-tuple-element.1242.psi, f32[5,4,16,128]{3,2,1,0:T(8,128)S(1)} %get-tuple-element.1243.outer, f32[4,16,128]{2,1,0:T(8,128)S(1)} %get-tuple-element.1244.keep, ...), custom_call_target="tpu_custom_call", output_to_operand_aliasing={{}: (2, {})} | custom-call | tf_op jit(solution)/shard_map/cond/branch_5_fun/inner/pallas_call | solution.py:684
  56.7 0.6 %collective-permute-done.146 = f32[5,16,128]{2,1,0:T(8,128)} collective-permute-done((f32[5,16,128]{2,1,0:T(8,128)S(1)}, f32[5,16,128]{2,1,0:T(8,128)}, u32[]{:S(2)}, u32[]{:S(2)}) %collective-permute-start.146) | collective-permute-done | bytes 40992 | tf_op jit(solution)/shard_map/cond/branch_5_fun/ppermute | solution.py:732
  57.3 1.7 %last.1 = f32[5,4,16,128]{3,2,1,0:T(8,128)} custom-call(s32[8]{0:T(128)S(1)} %stack.55.flags, f32[5,4,16,128]{3,2,1,0:T(8,128)S(1)} %get-tuple-element.1375.base, f32[5,16,128]{2,1,0:T(8,128)S(1)} %get-tuple-element.1370.strip, f32[5,16,128]{2,1,0:T(8,128)} %get-tuple-element.1376.from_a, f32[5,16,128]{2,1,0:T(8,128)} %get-tuple-element.1377.from_b, ...), custom_call_target="tpu_custom_call" | custom-call | tf_op jit(solution)/shard_map/last/pallas_call | solution.py:684
  (29 shorter events, 0.6 us)
Async XLA Ops:
  0.0 0.9 %copy-start.1 = (f32[5,4,16,128]{3,2,1,0:T(8,128)S(1)}, f32[5,4,16,128]{3,2,1,0:T(8,128)}, u32[]{:S(2)}) copy-start(f32[5,4,16,128]{3,2,1,0:T(8,128)} %flow.3) | copy-start | bytes 491524
  0.0 2.1 %copy-start = (f32[2,5,4,16,128]{4,3,2,1,0:T(8,128)S(1)}, f32[2,5,4,16,128]{4,3,2,1,0:T(8,128)}, u32[]{:S(2)}) copy-start(f32[2,5,4,16,128]{4,3,2,1,0:T(8,128)} %param.41) | copy-start | bytes 983044
  2.1 13.8 %collective-permute-start.27 = (f32[5,24,128]{2,1,0:T(8,128)S(1)}, f32[5,24,128]{2,1,0:T(8,128)}, u32[]{:S(2)}, u32[]{:S(2)}) collective-permute-start(f32[5,24,128]{2,1,0:T(8,128)S(1)} %get-tuple-element.900), channel_id=1, source_target_pairs={{0,1},{4,5},{8,9},{12,13},{16,17},{20,21},{24,25},{28,29},{1,0},{5... | collective-permute-start | bytes 184328 | tf_op jit(solution)/shard_map/cond/branch_5_fun/ppermute | solution.py:732
  2.2 13.8 %collective-permute-start.26 = (f32[5,24,128]{2,1,0:T(8,128)S(1)}, f32[5,24,128]{2,1,0:T(8,128)}, u32[]{:S(2)}, u32[]{:S(2)}) collective-permute-start(f32[5,24,128]{2,1,0:T(8,128)S(1)} %get-tuple-element.899), channel_id=1, source_target_pairs={{0,28},{4,8},{8,4},{12,16},{16,12},{20,24},{24,20},{28,0},{1,29},{... | collective-permute-start | bytes 184328 | tf_op jit(solution)/shard_map/cond/branch_5_fun/ppermute | solution.py:732
  4.4 11.6 %collective-permute-start.25 = (f32[5,24,128]{2,1,0:T(8,128)S(1)}, f32[5,24,128]{2,1,0:T(8,128)}, u32[]{:S(2)}, u32[]{:S(2)}) collective-permute-start(f32[5,24,128]{2,1,0:T(8,128)S(1)} %get-tuple-element.899), channel_id=1, source_target_pairs={{0,4},{4,0},{8,12},{12,8},{16,20},{20,16},{24,28},{28,24},{1,5},{5... | collective-permute-start | bytes 184328 | tf_op jit(solution)/shard_map/cond/branch_5_fun/ppermute | solution.py:732
  4.9 11.1 %collective-permute-start.29 = (f32[5,24,128]{2,1,0:T(8,128)S(1)}, f32[5,24,128]{2,1,0:T(8,128)}, u32[]{:S(2)}, u32[]{:S(2)}) collective-permute-start(f32[5,24,128]{2,1,0:T(8,128)S(1)} %get-tuple-element.901), channel_id=1, source_target_pairs={{0,0},{4,4},{8,8},{12,12},{16,16},{20,20},{24,24},{28,28},{1,26},{... | collective-permute-start | bytes 184328 | tf_op jit(solution)/shard_map/cond/branch_5_fun/ppermute | solution.py:732
  9.6 7.7 %collective-permute-start.28 = (f32[5,24,128]{2,1,0:T(8,128)S(1)}, f32[5,24,128]{2,1,0:T(8,128)}, u32[]{:S(2)}, u32[]{:S(2)}) collective-permute-start(f32[5,24,128]{2,1,0:T(8,128)S(1)} %get-tuple-element.901), channel_id=1, source_target_pairs={{0,0},{4,4},{8,8},{12,12},{16,16},{20,20},{24,24},{28,28},{1,22},{... | collective-permute-start | bytes 184328 | tf_op jit(solution)/shard_map/cond/branch_5_fun/ppermute | solution.py:732
  20.9 9.5 %collective-permute-start.67 = (f32[5,8,128]{2,1,0:T(8,128)S(1)}, f32[5,8,128]{2,1,0:T(8,128)S(1)}, u32[]{:S(2)}, u32[]{:S(2)}) collective-permute-start(f32[5,8,128]{2,1,0:T(8,128)S(1)} %get-tuple-element.1031), channel_id=1, source_target_pairs={{0,1},{4,5},{8,9},{12,13},{16,17},{20,21},{24,25},{28,29},{1,0},{5... | collective-permute-start | bytes 61448 | tf_op jit(solution)/shard_map/cond/branch_5_fun/ppermute | solution.py:732
  21.0 9.4 %collective-permute-start.69 = (f32[5,8,128]{2,1,0:T(8,128)S(1)}, f32[5,8,128]{2,1,0:T(8,128)S(1)}, u32[]{:S(2)}, u32[]{:S(2)}) collective-permute-start(f32[5,8,128]{2,1,0:T(8,128)S(1)} %get-tuple-element.1032), channel_id=1, source_target_pairs={{0,0},{4,4},{8,8},{12,12},{16,16},{20,20},{24,24},{28,28},{1,22},{... | collective-permute-start | bytes 61448 | tf_op jit(solution)/shard_map/cond/branch_5_fun/ppermute | solution.py:732
  24.5 6.3 %collective-permute-start.68 = (f32[5,8,128]{2,1,0:T(8,128)S(1)}, f32[5,8,128]{2,1,0:T(8,128)S(1)}, u32[]{:S(2)}, u32[]{:S(2)}) collective-permute-start(f32[5,8,128]{2,1,0:T(8,128)S(1)} %get-tuple-element.1032), channel_id=1, source_target_pairs={{0,0},{4,4},{8,8},{12,12},{16,16},{20,20},{24,24},{28,28},{1,26},{... | collective-permute-start | bytes 61448 | tf_op jit(solution)/shard_map/cond/branch_5_fun/ppermute | solution.py:732
  26.7 4.1 %collective-permute-start.66 = (f32[5,16,128]{2,1,0:T(8,128)S(1)}, f32[5,16,128]{2,1,0:T(8,128)}, u32[]{:S(2)}, u32[]{:S(2)}) collective-permute-start(f32[5,16,128]{2,1,0:T(8,128)S(1)} %get-tuple-element.1030), channel_id=1, source_target_pairs={{0,28},{4,8},{8,4},{12,16},{16,12},{20,24},{24,20},{28,0},{1,29},{... | collective-permute-start | bytes 122888 | tf_op jit(solution)/shard_map/cond/branch_5_fun/ppermute | solution.py:732
  27.7 3.2 %collective-permute-start.65 = (f32[5,16,128]{2,1,0:T(8,128)S(1)}, f32[5,16,128]{2,1,0:T(8,128)}, u32[]{:S(2)}, u32[]{:S(2)}) collective-permute-start(f32[5,16,128]{2,1,0:T(8,128)S(1)} %get-tuple-element.1030), channel_id=1, source_target_pairs={{0,4},{4,0},{8,12},{12,8},{16,20},{20,16},{24,28},{28,24},{1,5},{5... | collective-permute-start | bytes 122888 | tf_op jit(solution)/shard_map/cond/branch_5_fun/ppermute | solution.py:732
  32.6 11.3 %collective-permute-start.107 = (f32[5,8,128]{2,1,0:T(8,128)S(1)}, f32[5,8,128]{2,1,0:T(8,128)S(1)}, u32[]{:S(2)}, u32[]{:S(2)}) collective-permute-start(f32[5,8,128]{2,1,0:T(8,128)S(1)} %get-tuple-element.1135), channel_id=1, source_target_pairs={{0,1},{4,5},{8,9},{12,13},{16,17},{20,21},{24,25},{28,29},{1,0},{5... | collective-permute-start | bytes 61448 | tf_op jit(solution)/shard_map/cond/branch_5_fun/ppermute | solution.py:732
  32.7 11.3 %collective-permute-start.109 = (f32[5,8,128]{2,1,0:T(8,128)S(1)}, f32[5,8,128]{2,1,0:T(8,128)S(1)}, u32[]{:S(2)}, u32[]{:S(2)}) collective-permute-start(f32[5,8,128]{2,1,0:T(8,128)S(1)} %get-tuple-element.1136), channel_id=1, source_target_pairs={{0,0},{4,4},{8,8},{12,12},{16,16},{20,20},{24,24},{28,28},{1,22},{... | collective-permute-start | bytes 61448 | tf_op jit(solution)/shard_map/cond/branch_5_fun/ppermute | solution.py:732
  37.7 6.4 %collective-permute-start.108 = (f32[5,8,128]{2,1,0:T(8,128)S(1)}, f32[5,8,128]{2,1,0:T(8,128)S(1)}, u32[]{:S(2)}, u32[]{:S(2)}) collective-permute-start(f32[5,8,128]{2,1,0:T(8,128)S(1)} %get-tuple-element.1136), channel_id=1, source_target_pairs={{0,0},{4,4},{8,8},{12,12},{16,16},{20,20},{24,24},{28,28},{1,26},{... | collective-permute-start | bytes 61448 | tf_op jit(solution)/shard_map/cond/branch_5_fun/ppermute | solution.py:732
  40.2 4.6 %collective-permute-start.106 = (f32[5,16,128]{2,1,0:T(8,128)S(1)}, f32[5,16,128]{2,1,0:T(8,128)}, u32[]{:S(2)}, u32[]{:S(2)}) collective-permute-start(f32[5,16,128]{2,1,0:T(8,128)S(1)} %get-tuple-element.1134), channel_id=1, source_target_pairs={{0,28},{4,8},{8,4},{12,16},{16,12},{20,24},{24,20},{28,0},{1,29},{... | collective-permute-start | bytes 122888 | tf_op jit(solution)/shard_map/cond/branch_5_fun/ppermute | solution.py:732
  41.3 3.5 %collective-permute-start.105 = (f32[5,16,128]{2,1,0:T(8,128)S(1)}, f32[5,16,128]{2,1,0:T(8,128)}, u32[]{:S(2)}, u32[]{:S(2)}) collective-permute-start(f32[5,16,128]{2,1,0:T(8,128)S(1)} %get-tuple-element.1134), channel_id=1, source_target_pairs={{0,4},{4,0},{8,12},{12,8},{16,20},{20,16},{24,28},{28,24},{1,5},{5... | collective-permute-start | bytes 122888 | tf_op jit(solution)/shard_map/cond/branch_5_fun/ppermute | solution.py:732
  46.8 9.9 %collective-permute-start.147 = (f32[5,8,128]{2,1,0:T(8,128)S(1)}, f32[5,8,128]{2,1,0:T(8,128)S(1)}, u32[]{:S(2)}, u32[]{:S(2)}) collective-permute-start(f32[5,8,128]{2,1,0:T(8,128)S(1)} %get-tuple-element.1239), channel_id=1, source_target_pairs={{0,1},{4,5},{8,9},{12,13},{16,17},{20,21},{24,25},{28,29},{1,0},{5... | collective-permute-start | bytes 61448 | tf_op jit(solution)/shard_map/cond/branch_5_fun/ppermute | solution.py:732
  46.9 9.8 %collective-permute-start.149 = (f32[5,8,128]{2,1,0:T(8,128)S(1)}, f32[5,8,128]{2,1,0:T(8,128)S(1)}, u32[]{:S(2)}, u32[]{:S(2)}) collective-permute-start(f32[5,8,128]{2,1,0:T(8,128)S(1)} %get-tuple-element.1240), channel_id=1, source_target_pairs={{0,0},{4,4},{8,8},{12,12},{16,16},{20,20},{24,24},{28,28},{1,22},{... | collective-permute-start | bytes 61448 | tf_op jit(solution)/shard_map/cond/branch_5_fun/ppermute | solution.py:732
  50.2 6.5 %collective-permute-start.148 = (f32[5,8,128]{2,1,0:T(8,128)S(1)}, f32[5,8,128]{2,1,0:T(8,128)S(1)}, u32[]{:S(2)}, u32[]{:S(2)}) collective-permute-start(f32[5,8,128]{2,1,0:T(8,128)S(1)} %get-tuple-element.1240), channel_id=1, source_target_pairs={{0,0},{4,4},{8,8},{12,12},{16,16},{20,20},{24,24},{28,28},{1,26},{... | collective-permute-start | bytes 61448 | tf_op jit(solution)/shard_map/cond/branch_5_fun/ppermute | solution.py:732
  53.3 4.0 %collective-permute-start.146 = (f32[5,16,128]{2,1,0:T(8,128)S(1)}, f32[5,16,128]{2,1,0:T(8,128)}, u32[]{:S(2)}, u32[]{:S(2)}) collective-permute-start(f32[5,16,128]{2,1,0:T(8,128)S(1)} %get-tuple-element.1238), channel_id=1, source_target_pairs={{0,28},{4,8},{8,4},{12,16},{16,12},{20,24},{24,20},{28,0},{1,29},{... | collective-permute-start | bytes 122888 | tf_op jit(solution)/shard_map/cond/branch_5_fun/ppermute | solution.py:732
  55.5 1.8 %collective-permute-start.145 = (f32[5,16,128]{2,1,0:T(8,128)S(1)}, f32[5,16,128]{2,1,0:T(8,128)}, u32[]{:S(2)}, u32[]{:S(2)}) collective-permute-start(f32[5,16,128]{2,1,0:T(8,128)S(1)} %get-tuple-element.1238), channel_id=1, source_target_pairs={{0,4},{4,0},{8,12},{12,8},{16,20},{20,16},{24,28},{28,24},{1,5},{5... | collective-permute-start | bytes 122888 | tf_op jit(solution)/shard_map/cond/branch_5_fun/ppermute | solution.py:732
